TPU v7x, 32 devices: a whole 2x2x4 slice. The times are simulated.
32 devices in a mesh: freq: 8 (over y, x, core), blk: 4 (over z).
Axes of the slice: x: 2, y: 2, z: 4, core: 2. Of those that a mesh axis runs over, the one named last changes fastest.
Arguments:
- traces: bfloat16 [32, 4096, 1024], P(('blk', 'freq')), may hold values from -6 to 6
- fir: float32 [128], replicated, may hold values from -0.5 to 0.5
- targets: int32 [256], replicated, may hold values from 0 to 31
- band: int32 [2], replicated, may hold values from 1 to 512, as said below
Outputs:
- multiples: float32 [32, 2, 256, 4096], P('freq', None, None, 'blk')
Inputs may be any that keep to these rules, and one draw needn't show every extreme that they name: band[1] is 512 and band[1] - band[0] is at least 256.
All inputs are finite; a program needn't handle non-finite values.
Results may differ from a plain program's by a relative error of at most 0.019.
Values may be sent and summed in bfloat16 or wider, within the bound.
A program may use at most 128 MiB of HBM per device.

v0:
```python
import functools
import math

import jax
import jax.numpy as jnp
from jax import lax
from jax.experimental import pallas as pl
from jax.experimental.pallas import tpu as pltpu
from jax.sharding import PartitionSpec as P

FREQ_DEV = 4
PARTS = 2 * FREQ_DEV
ROWS = 2 * PARTS
VMEM_LIMIT = 56 * 2**20
MESH = pl.DeviceIdType.MESH


def dot(a, b, dims=(((1,), (0,)), ((), ())), precision=None):
    return lax.dot_general(a, b, dims, precision=precision, preferred_element_type=jnp.float32)


def cos_turns(turns):
    w = (0.25 - jnp.abs(turns - 0.5)) * (2.0 * math.pi)
    w2 = w * w
    total = jnp.full_like(w, 1.0 / math.factorial(13))
    for order in (11, 9, 7, 5, 3, 1):
        sign = 1.0 if order % 4 == 1 else -1.0
        total = total * w2 + sign / math.factorial(order)
    return -(total * w)


def flipped(index, offset, count):
    total = 0
    bit = 1
    while bit < count:
        total = total + bit * lax.rem(index // bit + (offset // bit) % 2, 2)
        bit *= 2
    return total


def send_kernel(
    freq_devs, blk_devs, col_stride,
    band_ref, fir_ref, traces_ref, recv_ref, plane_ref,
    traces_buf, spots_buf, table, outgoing, near_out, near_in, plane_out,
    chunk_sem, spot_sem, own_sem, send_sem, recv_sem,
    near_send, near_recv, plane_own, plane_send, plane_recv,
):
    me_f = lax.axis_index("freq")
    me_b = lax.axis_index("blk")
    me = me_b * freq_devs + me_f
    n = freq_devs * blk_devs
    spots, _, time_count = traces_buf.shape
    rec_count = spots * col_stride
    width = rec_count // blk_devs
    half = width // 2
    freq_count = FREQ_DEV * freq_devs
    cols = 2 * freq_count
    taps = fir_ref.shape[1]
    per = width // col_stride
    _, near_rows, near_lanes = near_out.shape
    packed = near_lanes // spots

    crossing = list(range(blk_devs // 2, blk_devs))
    offsets = crossing + list(range(blk_devs // 2 - 1, -1, -1))

    def spot_copy():
        return pltpu.make_async_copy(
            traces_ref.at[:, pl.ds(0, 16), :], spots_buf, spot_sem
        )

    def chunk_copy(step):
        block = flipped(me_b, offsets[step], blk_devs)
        return pltpu.make_async_copy(
            traces_ref.at[pl.ds(block * per, per)],
            traces_buf.at[pl.ds(step * per, per)],
            chunk_sem.at[step],
        )

    chunk_copy(0).start()
    spot_copy().start()
    for step in range(1, blk_devs):
        chunk_copy(step).start()

    barrier = pltpu.get_barrier_semaphore()

    @pl.loop(1, n)
    def _(d):
        to = lax.rem(me + d, n)
        pl.semaphore_signal(
            barrier, inc=1, device_id=(lax.rem(to, freq_devs), to // freq_devs), device_id_type=MESH
        )

    row = lax.broadcasted_iota(jnp.int32, (cols, time_count), 0)
    time = lax.broadcasted_iota(jnp.int32, (cols, time_count), 1)
    period = freq_count * time_count
    low = band_ref[0]
    high = band_ref[1]
    numerator = low * freq_count + (high - low) * (row >> 1)
    turn = numerator * time

    def cosine(shift):
        return cos_turns(((turn + shift) & (period - 1)).astype(jnp.float32) * (1.0 / period))

    quarter = period // 4
    part = (row & 1) * quarter
    cos_full = cosine(part)
    sin_full = cosine(part + 3 * quarter)
    head = turn[:, :taps]
    lag = lax.broadcasted_iota(jnp.int32, (taps, taps), 0)
    late = lax.broadcasted_iota(jnp.int32, (taps, taps), 1)
    kept = jnp.where(lag < taps - late, 1.0, 0.0).astype(jnp.float32)
    fir = fir_ref[...]
    scale = 1.0 / math.sqrt(time_count)

    def head_cos(shift):
        return cos_turns(((head + shift) & (period - 1)).astype(jnp.float32) * (1.0 / period))

    sum_cos = dot(head_cos(0) * fir, kept, precision=lax.Precision.HIGHEST) * scale
    sum_sin = dot(head_cos(3 * quarter) * fir, kept, precision=lax.Precision.HIGHEST) * scale
    body = time_count - taps
    mixed = jnp.concatenate(
        [
            cos_full[:, :body] * sum_cos[:, :1] - sin_full[:, :body] * sum_sin[:, :1],
            cos_full[:, body:] * sum_cos - sin_full[:, body:] * sum_sin,
        ],
        1,
    )
    mixed_high = mixed.astype(jnp.bfloat16)
    mixed_low = mixed - mixed_high.astype(jnp.float32)
    table[...] = (
        jnp.concatenate([mixed_high.astype(jnp.float32), mixed_low], 0).T.astype(jnp.bfloat16)
    )

    def spectrum_of(rows):
        both = dot(rows, table[...]).T
        return both[:cols] + both[cols:]


    def near_copy(f, slot):
        return pltpu.make_async_remote_copy(
            src_ref=near_out.at[f],
            dst_ref=near_in.at[slot],
            send_sem=near_send.at[f],
            recv_sem=near_recv.at[slot],
            device_id=(f, me_b),
            device_id_type=MESH,
        )

    def plane_copy(offset, slot):
        return pltpu.make_async_remote_copy(
            src_ref=plane_out,
            dst_ref=plane_ref.at[slot],
            send_sem=plane_send.at[offset],
            recv_sem=plane_recv.at[slot],
            device_id=(me_f, flipped(me_b, offset, blk_devs)),
            device_id_type=MESH,
        )

    own_plane = pltpu.make_async_copy(plane_out, plane_ref.at[me_b], plane_own)

    def remote(step, f):
        block = flipped(me_b, offsets[step], blk_devs)
        return pltpu.make_async_remote_copy(
            src_ref=outgoing.at[step, f],
            dst_ref=recv_ref.at[me],
            send_sem=send_sem.at[step * freq_devs + f],
            recv_sem=recv_sem.at[me],
            device_id=(f, block),
            device_id_type=MESH,
        )

    own = pltpu.make_async_copy(outgoing.at[blk_devs - 1, me_f], recv_ref.at[me], own_sem)
    for step in range(blk_devs):
        chunk_copy(step).wait()
        values = spectrum_of(
            traces_buf[pl.ds(step * per, per)].reshape(width, time_count)
        )
        values = values.reshape(freq_devs, PARTS, width)
        values = jnp.concatenate([values[:, :, :half], values[:, :, half:]], 1)
        outgoing[step] = values.astype(jnp.bfloat16)
        if step == 0:
            pl.semaphore_wait(barrier, n - 1)
        first = 0
        if step == blk_devs - 1:
            own.start()
            first = 1

        @pl.loop(first, freq_devs)
        def _(d):
            remote(step, lax.rem(me_f + d, freq_devs)).start()

        if step == 0:
            spot_copy().wait()
            near = spectrum_of(spots_buf[...].reshape(spots * 16, time_count)).astype(jnp.bfloat16)
            spot_row = lax.broadcasted_iota(jnp.int32, (spots * 16, near_lanes), 0)
            spot_col = lax.broadcasted_iota(jnp.int32, (spots * 16, near_lanes), 1)
            shift = lax.rem(me_f, packed) * spots
            pick = jnp.where(spot_row == (spot_col - shift) * 16, 1.0, 0.0).astype(jnp.bfloat16)
            at_spots = dot(near, pick).reshape(freq_devs, PARTS, near_lanes)
            at_spots = jnp.concatenate([at_spots] * (near_rows // PARTS), 1)
            line = lax.broadcasted_iota(jnp.int32, at_spots.shape, 1) // PARTS
            near_out[...] = jnp.where(line == me_f // packed, at_spots, 0.0).astype(jnp.bfloat16)

            @pl.loop(1, freq_devs)
            def _(d):
                near_copy(lax.rem(me_f + d, freq_devs), me_f).start()

        if step == blk_devs - 2:
            total = near_out[me_f].astype(jnp.float32)
            for d in range(1, freq_devs):
                source = lax.rem(me_f + d, freq_devs)
                near_copy(source, source).wait_recv()
                total = total + near_in[source].astype(jnp.float32)
            plane_out[...] = total.astype(jnp.bfloat16)
            own_plane.start()
            for offset in range(1, blk_devs):
                plane_copy(offset, me_b).start()

    own.wait()
    own_plane.wait()

    @pl.loop(1, freq_devs)
    def _(d):
        near_copy(lax.rem(me_f + d, freq_devs), me_f).wait_send()

    for offset in range(1, blk_devs):
        plane_copy(offset, me_b).wait_send()
        plane_copy(offset, flipped(me_b, offset, blk_devs)).wait_recv()
    for step in range(blk_devs):

        @pl.loop(1 if step == blk_devs - 1 else 0, freq_devs)
        def _(d):
            remote(step, lax.rem(me_f + d, freq_devs)).wait_send()

    @pl.loop(1, n)
    def _(d):
        source = lax.rem(me + d, n)
        pltpu.make_async_remote_copy(
            src_ref=outgoing.at[0, 0],
            dst_ref=recv_ref.at[source],
            send_sem=send_sem.at[0],
            recv_sem=recv_sem.at[source],
            device_id=(lax.rem(source, freq_devs), source // freq_devs),
            device_id_type=MESH,
        ).wait_recv()


def product_kernel(freq_devs, targets_ref, recv_ref, plane_ref, out_ref, made, sems):
    shots, rows, lanes = recv_ref.shape
    blk_devs, near_rows, near_lanes = plane_ref.shape
    packed = near_lanes // shots
    half = made.shape[3] // 2
    depth = shots * rows
    count = targets_ref.shape[1]

    wanted = jnp.broadcast_to(targets_ref[...].astype(jnp.float32), (128, count)).T
    shot = lax.broadcasted_iota(jnp.int32, (count, 2 * shots), 1)
    shot = jnp.where(shot >= shots, shot - shots, shot)
    chooser = jnp.where(shot == wanted[:, :1].astype(jnp.int32), 1.0, 0.0).astype(jnp.bfloat16)
    fold_row = lax.broadcasted_iota(jnp.int32, (near_lanes, max(128, 2 * shots)), 0)
    fold_col = lax.broadcasted_iota(jnp.int32, (near_lanes, max(128, 2 * shots)), 1)
    fold = jnp.where(fold_row % shots == fold_col % shots, 1.0, 0.0).astype(jnp.bfloat16)
    scale = 1.0 / math.sqrt(shots)

    def write(i, o):
        return pltpu.make_async_copy(made.at[i, o], out_ref.at[i, o], sems.at[i, o])

    for i in range(FREQ_DEV):
        line = lax.broadcasted_iota(jnp.int32, (4 * shots, depth), 0)
        place = lax.broadcasted_iota(jnp.int32, (4 * shots, depth), 1)
        group = line // shots
        home = (line - group * shots) * rows + (group // 2) * PARTS + (group & 1) + 2 * i
        pick = jnp.where(place == home, 1.0, 0.0).astype(jnp.bfloat16)
        picked = dot(pick, recv_ref[...].reshape(depth, lanes))

        near_depth = blk_devs * near_rows
        line = lax.broadcasted_iota(jnp.int32, (2 * shots, near_depth), 0)
        place = lax.broadcasted_iota(jnp.int32, (2 * shots, near_depth), 1)
        part = line // shots
        from_shot = line - part * shots
        from_f = from_shot % freq_devs
        home = (from_shot // freq_devs) * near_rows + (from_f // packed) * PARTS + 2 * i + part
        pick = jnp.where(place == home, 1.0, 0.0).astype(jnp.bfloat16)
        near = dot(pick, plane_ref[...].reshape(near_depth, near_lanes))
        slot = lax.broadcasted_iota(jnp.int32, near.shape, 0) % freq_devs % packed
        lane = lax.broadcasted_iota(jnp.int32, near.shape, 1)
        near = jnp.where(lane // shots == slot, near, 0.0).astype(jnp.bfloat16)
        near = dot(near, fold)
        source = lax.broadcasted_iota(jnp.int32, near.shape, 0) >= shots
        lane = lax.broadcasted_iota(jnp.int32, near.shape, 1)
        target = lane >= shots
        inside = lane < 2 * shots
        same = inside & (source == target)
        other = inside & (source != target)
        parts = [
            jnp.where(same, jnp.where(source, -near, near), 0.0),
            jnp.where(other, near, 0.0),
        ]
        lefts = [dot(chooser, p.astype(jnp.bfloat16)).astype(jnp.bfloat16) for p in parts]
        rights = [
            picked[2 * shots * h : 2 * shots * (h + 1), :half].astype(jnp.bfloat16) for h in range(2)
        ]
        for o in range(2):
            for h in range(2):
                made[i, o, :, pl.ds(h * half, half)] = dot(lefts[o][:, : 2 * shots], rights[h]) * scale
            write(i, o).start()

    for i in range(FREQ_DEV):
        for o in range(2):
            write(i, o).wait()


def per_device(traces, fir, targets, band):
    shot_dev, rec_count, time_count = traces.shape
    freq_devs = lax.axis_size("freq")
    blk_devs = lax.axis_size("blk")
    n = freq_devs * blk_devs
    assert shot_dev == 1
    assert blk_devs & (blk_devs - 1) == 0
    col_stride = rec_count // n
    width = rec_count // blk_devs
    half = width // 2
    lanes = half
    near_lanes = max(128, n)
    packed = near_lanes // n
    near_rows = freq_devs // packed * PARTS
    cols = 2 * FREQ_DEV * freq_devs
    received, planes = pl.pallas_call(
        functools.partial(send_kernel, freq_devs, blk_devs, col_stride),
        out_shape=[
            jax.ShapeDtypeStruct((n, ROWS, lanes), jnp.bfloat16),
            jax.ShapeDtypeStruct((blk_devs, near_rows, near_lanes), jnp.bfloat16),
        ],
        in_specs=[
            pl.BlockSpec(memory_space=pltpu.SMEM),
            pl.BlockSpec(memory_space=pltpu.VMEM),
            pl.BlockSpec(memory_space=pl.ANY),
        ],
        out_specs=[pl.BlockSpec(memory_space=pl.ANY)] * 2,
        scratch_shapes=[
            pltpu.VMEM((n, col_stride, time_count), jnp.bfloat16),
            pltpu.VMEM((n, 16, time_count), jnp.bfloat16),
            pltpu.VMEM((time_count, 2 * cols), jnp.bfloat16),
            pltpu.VMEM((blk_devs, freq_devs, ROWS, lanes), jnp.bfloat16),
            pltpu.VMEM((freq_devs, near_rows, near_lanes), jnp.bfloat16),
            pltpu.VMEM((freq_devs, near_rows, near_lanes), jnp.bfloat16),
            pltpu.VMEM((near_rows, near_lanes), jnp.bfloat16),
            pltpu.SemaphoreType.DMA((blk_devs,)),
            pltpu.SemaphoreType.DMA,
            pltpu.SemaphoreType.DMA,
            pltpu.SemaphoreType.DMA((n,)),
            pltpu.SemaphoreType.DMA((n,)),
            pltpu.SemaphoreType.DMA((freq_devs,)),
            pltpu.SemaphoreType.DMA((freq_devs,)),
            pltpu.SemaphoreType.DMA,
            pltpu.SemaphoreType.DMA((blk_devs,)),
            pltpu.SemaphoreType.DMA((blk_devs,)),
        ],
        compiler_params=pltpu.CompilerParams(
            collective_id=0, has_side_effects=True, vmem_limit_bytes=VMEM_LIMIT
        ),
    )(band, fir.reshape(1, -1), traces.reshape(n, col_stride, time_count))
    count = targets.shape[0]
    return pl.pallas_call(
        functools.partial(product_kernel, freq_devs),
        out_shape=jax.ShapeDtypeStruct((FREQ_DEV, 2, count, width), jnp.float32),
        in_specs=[pl.BlockSpec(memory_space=pltpu.VMEM)] * 3,
        out_specs=pl.BlockSpec(memory_space=pl.ANY),
        scratch_shapes=[
            pltpu.VMEM((FREQ_DEV, 2, count, width), jnp.float32),
            pltpu.SemaphoreType.DMA((FREQ_DEV, 2)),
        ],
        compiler_params=pltpu.CompilerParams(vmem_limit_bytes=VMEM_LIMIT),
    )(targets.reshape(1, -1), received, planes)


def solution(mesh):
    placed = (P(("blk", "freq"), None, None), P(), P(), P())
    return jax.shard_map(
        per_device,
        mesh=mesh,
        in_specs=placed,
        out_specs=P("freq", None, None, "blk"),
        check_vma=False,
    )
```

profile of v0, /device:TPU:0, one launch (start us, length us, event | category | flops | bytes accessed | tf_op | source)
XLA Modules:
  0.0 28.0 jit_solution(1613278847005954008)
XLA Ops:
  0.0 22.7 %shard_map.46 = (bf16[32,16,512]{2,1,0:T(8,128)(2,1)}, bf16[4,16,128]{2,1,0:T(8,128)(2,1)}) custom-call(s32[2]{0:T(128)} %band_ref.1, f32[1,128]{1,0:T(1,128)} %bitcast.5, bf16[32,128,1024]{2,1,0:T(8,128)(2,1)} %bitcast.3), custom_call_target="tpu_custom_call" | custom-call | tf_op jit(solution)/shard_map/pallas_call | solution.py:328
  22.7 5.3 %shard_map.47 = f32[4,2,256,1024]{3,2,1,0:T(8,128)} custom-call(s32[1,256]{1,0:T(1,128)} %bitcast.4, bf16[32,16,512]{2,1,0:T(8,128)(2,1)} %get-tuple-element.7.recv_ref, bf16[4,16,128]{2,1,0:T(8,128)(2,1)} %get-tuple-element.8.plane_ref), custom_call_target="tpu_custom_call" | custom-call | tf_op jit(solution)/shard_map/pallas_call | solution.py:364
where the time goes:
time: 28.2 us; the launch traced here: 28 us
  Pallas kernels  28 us (99%)
    pallas_call x1, Pallas kernels, per_device(): pl.pallas_call(functools.partial(send_kernel, freq_devs, blk_devs, col_st...  22.7 us
    pallas_call x1, Pallas kernels, per_device(): pl.pallas_call(functools.partial(product_kernel, freq_devs), out_shape=ja...  5.3 us

commit v1 on v0

--- a/solution.py
+++ b/solution.py
@@ -11,7 +11,8 @@
 FREQ_DEV = 4
 PARTS = 2 * FREQ_DEV
 ROWS = 2 * PARTS
-VMEM_LIMIT = 56 * 2**20
+VMEM_LIMIT = 40 * 2**20
+GROUP = 32
 MESH = pl.DeviceIdType.MESH
 
 
@@ -40,9 +41,10 @@
 
 def send_kernel(
     freq_devs, blk_devs, col_stride,
-    band_ref, fir_ref, traces_ref, recv_ref, plane_ref,
-    traces_buf, spots_buf, table, outgoing, near_out, near_in, plane_out,
-    chunk_sem, spot_sem, own_sem, send_sem, recv_sem,
+    band_hbm, fir_hbm, targets_hbm, traces_ref, recv_ref, left_ref, sort_ref,
+    band_ref, fir_ref, targets_ref,
+    traces_buf, spots_buf, table, outgoing, near_out, near_in, plane_out, plane_ref,
+    small_sem, chunk_sem, spot_sem, own_sem, send_sem, recv_sem,
     near_send, near_recv, plane_own, plane_send, plane_recv,
 ):
     me_f = lax.axis_index("freq")
@@ -76,11 +78,13 @@
             chunk_sem.at[step],
         )
 
+    small = [
+        pltpu.make_async_copy(band_hbm, band_ref, small_sem.at[0]),
+        pltpu.make_async_copy(fir_hbm, fir_ref, small_sem.at[1]),
+        pltpu.make_async_copy(targets_hbm, targets_ref, small_sem.at[2]),
+    ]
+    small[0].start()
     chunk_copy(0).start()
-    spot_copy().start()
-    for step in range(1, blk_devs):
-        chunk_copy(step).start()
-
     barrier = pltpu.get_barrier_semaphore()
 
     @pl.loop(1, n)
@@ -89,6 +93,14 @@
         pl.semaphore_signal(
             barrier, inc=1, device_id=(lax.rem(to, freq_devs), to // freq_devs), device_id_type=MESH
         )
+
+    small[1].start()
+    small[2].start()
+    spot_copy().start()
+    for step in range(1, blk_devs):
+        chunk_copy(step).start()
+    small[0].wait()
+    small[1].wait()
 
     row = lax.broadcasted_iota(jnp.int32, (cols, time_count), 0)
     time = lax.broadcasted_iota(jnp.int32, (cols, time_count), 1)
@@ -216,8 +228,14 @@
             for offset in range(1, blk_devs):
                 plane_copy(offset, me_b).start()
 
+    rows = recv_ref.shape[1]
+    fill_sort(sort_ref, rows)
+    own_plane.wait()
+    for offset in range(1, blk_devs):
+        plane_copy(offset, flipped(me_b, offset, blk_devs)).wait_recv()
+    small[2].wait()
+    fill_left(freq_devs, targets_ref, plane_ref, left_ref)
     own.wait()
-    own_plane.wait()
 
     @pl.loop(1, freq_devs)
     def _(d):
@@ -225,7 +243,6 @@
 
     for offset in range(1, blk_devs):
         plane_copy(offset, me_b).wait_send()
-        plane_copy(offset, flipped(me_b, offset, blk_devs)).wait_recv()
     for step in range(blk_devs):
 
         @pl.loop(1 if step == blk_devs - 1 else 0, freq_devs)
@@ -245,35 +262,32 @@
         ).wait_recv()
 
 
-def product_kernel(freq_devs, targets_ref, recv_ref, plane_ref, out_ref, made, sems):
-    shots, rows, lanes = recv_ref.shape
+def fill_sort(sort_ref, rows):
+    lines, depth = sort_ref.shape
+    half = rows // 2
+    line = lax.broadcasted_iota(jnp.int32, (lines, depth), 0)
+    place = lax.broadcasted_iota(jnp.int32, (lines, depth), 1)
+    group = line // GROUP
+    home = (line % GROUP) * rows + (group // 2) % 2 * half + group // 4 * 2 + group % 2
+    sort_ref[...] = jnp.where(place == home, 1.0, 0.0).astype(jnp.bfloat16)
+
+
+def fill_left(freq_devs, targets_ref, plane_ref, left_ref):
     blk_devs, near_rows, near_lanes = plane_ref.shape
+    shots = left_ref.shape[2] // 2
     packed = near_lanes // shots
-    half = made.shape[3] // 2
-    depth = shots * rows
     count = targets_ref.shape[1]
-
+    wide = max(128, 2 * shots)
     wanted = jnp.broadcast_to(targets_ref[...].astype(jnp.float32), (128, count)).T
     shot = lax.broadcasted_iota(jnp.int32, (count, 2 * shots), 1)
     shot = jnp.where(shot >= shots, shot - shots, shot)
     chooser = jnp.where(shot == wanted[:, :1].astype(jnp.int32), 1.0, 0.0).astype(jnp.bfloat16)
-    fold_row = lax.broadcasted_iota(jnp.int32, (near_lanes, max(128, 2 * shots)), 0)
-    fold_col = lax.broadcasted_iota(jnp.int32, (near_lanes, max(128, 2 * shots)), 1)
-    fold = jnp.where(fold_row % shots == fold_col % shots, 1.0, 0.0).astype(jnp.bfloat16)
-    scale = 1.0 / math.sqrt(shots)
-
-    def write(i, o):
-        return pltpu.make_async_copy(made.at[i, o], out_ref.at[i, o], sems.at[i, o])
-
+    fold_row = lax.broadcasted_iota(jnp.int32, (near_lanes, wide), 0)
+    fold_col = lax.broadcasted_iota(jnp.int32, (near_lanes, wide), 1)
+    fold_spot = fold_col // (2 * GROUP) * GROUP + fold_col % GROUP
+    fold = jnp.where(fold_row % shots == fold_spot % shots, 1.0, 0.0).astype(jnp.bfloat16)
+    near_depth = blk_devs * near_rows
     for i in range(FREQ_DEV):
-        line = lax.broadcasted_iota(jnp.int32, (4 * shots, depth), 0)
-        place = lax.broadcasted_iota(jnp.int32, (4 * shots, depth), 1)
-        group = line // shots
-        home = (line - group * shots) * rows + (group // 2) * PARTS + (group & 1) + 2 * i
-        pick = jnp.where(place == home, 1.0, 0.0).astype(jnp.bfloat16)
-        picked = dot(pick, recv_ref[...].reshape(depth, lanes))
-
-        near_depth = blk_devs * near_rows
         line = lax.broadcasted_iota(jnp.int32, (2 * shots, near_depth), 0)
         place = lax.broadcasted_iota(jnp.int32, (2 * shots, near_depth), 1)
         part = line // shots
@@ -288,7 +302,7 @@
         near = dot(near, fold)
         source = lax.broadcasted_iota(jnp.int32, near.shape, 0) >= shots
         lane = lax.broadcasted_iota(jnp.int32, near.shape, 1)
-        target = lane >= shots
+        target = lane // GROUP % 2 == 1
         inside = lane < 2 * shots
         same = inside & (source == target)
         other = inside & (source != target)
@@ -296,13 +310,36 @@
             jnp.where(same, jnp.where(source, -near, near), 0.0),
             jnp.where(other, near, 0.0),
         ]
-        lefts = [dot(chooser, p.astype(jnp.bfloat16)).astype(jnp.bfloat16) for p in parts]
+        for o in range(2):
+            left = dot(chooser, parts[o].astype(jnp.bfloat16)).astype(jnp.bfloat16)
+            left_ref[i, pl.ds(o * count, count), :] = left[:, : 2 * shots]
+
+
+def product_kernel(recv_ref, left_ref, sort_ref, out_ref, made, sems):
+    shots, rows, half = recv_ref.shape
+    count = left_ref.shape[1] // 2
+    span = GROUP * rows
+    scale = 1.0 / math.sqrt(shots)
+
+    def write(i, o):
+        return pltpu.make_async_copy(
+            made.at[i, pl.ds(o * count, count)], out_ref.at[i, o], sems.at[i, o]
+        )
+
+    for i in range(FREQ_DEV):
+        lines = sort_ref[pl.ds(i * 4 * GROUP, 4 * GROUP), :]
         rights = [
-            picked[2 * shots * h : 2 * shots * (h + 1), :half].astype(jnp.bfloat16) for h in range(2)
+            dot(lines, recv_ref[pl.ds(g * GROUP, GROUP)].reshape(span, half)).astype(jnp.bfloat16)
+            for g in range(shots // GROUP)
+        ]
+        rights = [
+            jnp.concatenate([r[2 * GROUP * h : 2 * GROUP * (h + 1)] for r in rights], 0)
+            for h in range(2)
         ]
         for o in range(2):
+            left = left_ref[i, pl.ds(o * count, count), :]
             for h in range(2):
-                made[i, o, :, pl.ds(h * half, half)] = dot(lefts[o][:, : 2 * shots], rights[h]) * scale
+                made[i, pl.ds(o * count, count), pl.ds(h * half, half)] = dot(left, rights[h]) * scale
             write(i, o).start()
 
     for i in range(FREQ_DEV):
@@ -325,19 +362,23 @@
     packed = near_lanes // n
     near_rows = freq_devs // packed * PARTS
     cols = 2 * FREQ_DEV * freq_devs
-    received, planes = pl.pallas_call(
+    count = targets.shape[0]
+    assert n % GROUP == 0
+    lines = 4 * FREQ_DEV * GROUP
+    hbm = lambda x: pltpu.with_memory_space_constraint(x, pltpu.HBM)
+    received, lefts, sorter = pl.pallas_call(
         functools.partial(send_kernel, freq_devs, blk_devs, col_stride),
         out_shape=[
-            jax.ShapeDtypeStruct((n, ROWS, lanes), jnp.bfloat16),
-            jax.ShapeDtypeStruct((blk_devs, near_rows, near_lanes), jnp.bfloat16),
+            pltpu.VMEM((n, ROWS, lanes), jnp.bfloat16),
+            pltpu.VMEM((FREQ_DEV, 2 * count, 2 * n), jnp.bfloat16),
+            pltpu.VMEM((lines, GROUP * ROWS), jnp.bfloat16),
         ],
-        in_specs=[
-            pl.BlockSpec(memory_space=pltpu.SMEM),
-            pl.BlockSpec(memory_space=pltpu.VMEM),
-            pl.BlockSpec(memory_space=pl.ANY),
-        ],
-        out_specs=[pl.BlockSpec(memory_space=pl.ANY)] * 2,
+        in_specs=[pl.BlockSpec(memory_space=pl.ANY)] * 4,
+        out_specs=[pl.BlockSpec(memory_space=pltpu.VMEM)] * 3,
         scratch_shapes=[
+            pltpu.SMEM((2,), jnp.int32),
+            pltpu.VMEM((1, fir.shape[0]), jnp.float32),
+            pltpu.VMEM((1, count), jnp.int32),
             pltpu.VMEM((n, col_stride, time_count), jnp.bfloat16),
             pltpu.VMEM((n, 16, time_count), jnp.bfloat16),
             pltpu.VMEM((time_count, 2 * cols), jnp.bfloat16),
@@ -345,6 +386,8 @@
             pltpu.VMEM((freq_devs, near_rows, near_lanes), jnp.bfloat16),
             pltpu.VMEM((freq_devs, near_rows, near_lanes), jnp.bfloat16),
             pltpu.VMEM((near_rows, near_lanes), jnp.bfloat16),
+            pltpu.VMEM((blk_devs, near_rows, near_lanes), jnp.bfloat16),
+            pltpu.SemaphoreType.DMA((3,)),
             pltpu.SemaphoreType.DMA((blk_devs,)),
             pltpu.SemaphoreType.DMA,
             pltpu.SemaphoreType.DMA,
@@ -359,19 +402,23 @@
         compiler_params=pltpu.CompilerParams(
             collective_id=0, has_side_effects=True, vmem_limit_bytes=VMEM_LIMIT
         ),
-    )(band, fir.reshape(1, -1), traces.reshape(n, col_stride, time_count))
-    count = targets.shape[0]
+    )(
+        hbm(band),
+        hbm(fir.reshape(1, -1)),
+        hbm(targets.reshape(1, -1)),
+        hbm(traces.reshape(n, col_stride, time_count)),
+    )
     return pl.pallas_call(
-        functools.partial(product_kernel, freq_devs),
+        product_kernel,
         out_shape=jax.ShapeDtypeStruct((FREQ_DEV, 2, count, width), jnp.float32),
         in_specs=[pl.BlockSpec(memory_space=pltpu.VMEM)] * 3,
         out_specs=pl.BlockSpec(memory_space=pl.ANY),
         scratch_shapes=[
-            pltpu.VMEM((FREQ_DEV, 2, count, width), jnp.float32),
+            pltpu.VMEM((FREQ_DEV, 2 * count, width), jnp.float32),
             pltpu.SemaphoreType.DMA((FREQ_DEV, 2)),
         ],
         compiler_params=pltpu.CompilerParams(vmem_limit_bytes=VMEM_LIMIT),
-    )(targets.reshape(1, -1), received, planes)
+    )(received, lefts, sorter)
 
 
 def solution(mesh):

time: 28.2 us -> 27.4 us (0.972)
  Pallas kernels: 28 us -> 27.3 us
    pallas_call x1, Pallas kernels: 5.3 us -> 3.85 us  [per_device(): pl.pallas_call(product_kernel, out_shape=jax.ShapeDtypeStruct((FREQ_DEV,...]
    pallas_call x1, Pallas kernels: 22.7 us -> 23.4 us  [per_device(): pl.pallas_call(functools.partial(send_kernel, freq_devs, blk_devs, col_st...]
where the time goes in v1:
time: 27.4 us; the launch traced here: 27.3 us
  Pallas kernels  27.3 us (100%)
    pallas_call x1, Pallas kernels, per_device(): pl.pallas_call(functools.partial(send_kernel, freq_devs, blk_devs, col_st...  23.4 us
    pallas_call x1, Pallas kernels, per_device(): pl.pallas_call(product_kernel, out_shape=jax.ShapeDtypeStruct((FREQ_DEV,...  3.85 us

profile of v1, /device:TPU:0, one launch (start us, length us, event | category | flops | bytes accessed | tf_op | source)
XLA Modules:
  0.0 27.3 jit_solution(17435708754665411738)
XLA Ops:
  0.0 23.4 %shard_map.46 = (bf16[32,16,512]{2,1,0:T(8,128)(2,1)S(1)}, bf16[4,512,64]{2,1,0:T(8,128)(2,1)S(1)}, bf16[512,512]{1,0:T(8,128)(2,1)S(1)}) custom-call(s32[2]{0:T(128)} %band_hbm.1, f32[1,128]{1,0:T(1,128)} %bitcast.5, s32[1,256]{1,0:T(1,128)} %bitcast.4, bf16[32,128,1024]{2,1,0:T(8,128)(2,1)} %bitcast.3), custom_call_target="tpu_custom_call" | custom-call | tf_op jit(solution)/shard_map/pallas_call | solution.py:369
  23.4 3.8 %shard_map.47 = f32[4,2,256,1024]{3,2,1,0:T(8,128)} custom-call(bf16[32,16,512]{2,1,0:T(8,128)(2,1)S(1)} %get-tuple-element.8.recv_ref, bf16[4,512,64]{2,1,0:T(8,128)(2,1)S(1)} %get-tuple-element.9.left_ref, bf16[512,512]{1,0:T(8,128)(2,1)S(1)} %get-tuple-element.10.sort_ref), custom_call_target="tpu_custom_call" | custom-call | tf_op jit(solution)/shard_map/pallas_call | solution.py:411

commit v2 on v1

--- a/solution.py
+++ b/solution.py
@@ -44,8 +44,8 @@
     band_hbm, fir_hbm, targets_hbm, traces_ref, recv_ref, left_ref, sort_ref,
     band_ref, fir_ref, targets_ref,
     traces_buf, spots_buf, table, outgoing, near_out, near_in, plane_out, plane_ref,
-    small_sem, chunk_sem, spot_sem, own_sem, send_sem, recv_sem,
-    near_send, near_recv, plane_own, plane_send, plane_recv,
+    small_sem, chunk_sem, spot_sem, send_sem, recv_sem,
+    near_send, near_recv, plane_send, plane_recv,
 ):
     me_f = lax.axis_index("freq")
     me_b = lax.axis_index("blk")
@@ -57,7 +57,6 @@
     half = width // 2
     freq_count = FREQ_DEV * freq_devs
     cols = 2 * freq_count
-    taps = fir_ref.shape[1]
     per = width // col_stride
     _, near_rows, near_lanes = near_out.shape
     packed = near_lanes // spots
@@ -78,188 +77,187 @@
             chunk_sem.at[step],
         )
 
+    def enter(d):
+        to = lax.rem(me + d, n)
+        pl.semaphore_signal(
+            barrier, inc=1, device_id=(lax.rem(to, freq_devs), to // freq_devs), device_id_type=MESH
+        )
+
+    def near_copy(f):
+        return pltpu.make_async_remote_copy(
+            src_ref=near_out.at[f],
+            dst_ref=near_in.at[me_f],
+            send_sem=near_send,
+            recv_sem=near_recv,
+            device_id=(f, me_b),
+            device_id_type=MESH,
+        )
+
+    def plane_copy(offset, slot):
+        return pltpu.make_async_remote_copy(
+            src_ref=plane_out,
+            dst_ref=plane_ref.at[slot],
+            send_sem=plane_send,
+            recv_sem=plane_recv,
+            device_id=(me_f, flipped(me_b, offset, blk_devs)),
+            device_id_type=MESH,
+        )
+
+    def remote(step, f):
+        block = flipped(me_b, offsets[step], blk_devs)
+        return pltpu.make_async_remote_copy(
+            src_ref=outgoing.at[step, f],
+            dst_ref=recv_ref.at[me],
+            send_sem=send_sem.at[step],
+            recv_sem=recv_sem,
+            device_id=(f, block),
+            device_id_type=MESH,
+        )
+
+    def arrived(ref, sem):
+        pltpu.make_async_copy(ref, ref, sem).wait()
+
     small = [
         pltpu.make_async_copy(band_hbm, band_ref, small_sem.at[0]),
         pltpu.make_async_copy(fir_hbm, fir_ref, small_sem.at[1]),
         pltpu.make_async_copy(targets_hbm, targets_ref, small_sem.at[2]),
     ]
-    small[0].start()
-    chunk_copy(0).start()
     barrier = pltpu.get_barrier_semaphore()
-
-    @pl.loop(1, n)
-    def _(d):
-        to = lax.rem(me + d, n)
-        pl.semaphore_signal(
-            barrier, inc=1, device_id=(lax.rem(to, freq_devs), to // freq_devs), device_id_type=MESH
-        )
-
-    small[1].start()
+    with jax.named_scope("signals"):
+        small[0].start()
+        small[1].start()
+        spot_copy().start()
+        pl.loop(1, n)(enter)
+    for step in range(blk_devs):
+        chunk_copy(step).start()
     small[2].start()
-    spot_copy().start()
-    for step in range(1, blk_devs):
-        chunk_copy(step).start()
-    small[0].wait()
-    small[1].wait()
-
-    row = lax.broadcasted_iota(jnp.int32, (cols, time_count), 0)
-    time = lax.broadcasted_iota(jnp.int32, (cols, time_count), 1)
+    with jax.named_scope("small_wait"):
+        small[0].wait()
+        small[1].wait()
+    with jax.named_scope("table"):
+        fill_table(band_ref, fir_ref, table, freq_count)
+
+    def spectrum_of(rows):
+        both = dot(table[...], rows, (((1,), (1,)), ((), ())))
+        return both[:cols] + both[cols:]
+
+    with jax.named_scope("spots"):
+        spot_copy().wait()
+        near = spectrum_of(spots_buf[...].reshape(spots * 16, time_count)).astype(jnp.bfloat16)
+        spot_row = lax.broadcasted_iota(jnp.int32, (spots * 16, near_lanes), 0)
+        spot_col = lax.broadcasted_iota(jnp.int32, (spots * 16, near_lanes), 1)
+        shift = lax.rem(me_f, packed) * spots
+        pick = jnp.where(spot_row == (spot_col - shift) * 16, 1.0, 0.0).astype(jnp.bfloat16)
+        at_spots = dot(near, pick).reshape(freq_devs, PARTS, near_lanes)
+        at_spots = jnp.concatenate([at_spots] * (near_rows // PARTS), 1)
+        line = lax.broadcasted_iota(jnp.int32, at_spots.shape, 1) // PARTS
+        near_out[...] = jnp.where(line == me_f // packed, at_spots, 0.0).astype(jnp.bfloat16)
+        near_in[me_f] = near_out[me_f]
+
+    for step in range(blk_devs):
+        with jax.named_scope(f"chunk{step}"):
+            chunk_copy(step).wait()
+            values = spectrum_of(traces_buf[pl.ds(step * per, per)].reshape(width, time_count))
+            values = values.reshape(freq_devs, PARTS, width)
+            values = jnp.concatenate([values[:, :, :half], values[:, :, half:]], 1)
+            outgoing[step] = values.astype(jnp.bfloat16)
+        if step == 0:
+            with jax.named_scope("barrier"):
+                pl.semaphore_wait(barrier, n - 1)
+
+            @pl.loop(1, freq_devs)
+            def _(d):
+                near_copy(lax.rem(me_f + d, freq_devs)).start()
+
+        if step == 1:
+            with jax.named_scope("plane"):
+                arrived(near_in.at[pl.ds(0, freq_devs - 1)], near_recv)
+                total = near_in[...].astype(jnp.float32)
+                plane_out[...] = jnp.sum(total, 0).astype(jnp.bfloat16)
+                plane_ref[me_b] = plane_out[...]
+            for offset in range(1, blk_devs):
+                plane_copy(offset, me_b).start()
+
+        first = 0
+        if step == blk_devs - 1:
+            recv_ref[me] = outgoing[step, me_f]
+            first = 1
+
+        with jax.named_scope("send"):
+
+            @pl.loop(first, freq_devs)
+            def _(d):
+                remote(step, lax.rem(me_f + d, freq_devs)).start()
+
+    with jax.named_scope("sort"):
+        fill_sort(sort_ref, recv_ref.shape[1])
+    with jax.named_scope("plane_wait"):
+        arrived(plane_ref.at[pl.ds(0, blk_devs - 1)], plane_recv)
+        small[2].wait()
+    with jax.named_scope("left"):
+        fill_left(freq_devs, targets_ref, plane_ref, left_ref)
+    with jax.named_scope("send_wait"):
+        arrived(near_in.at[pl.ds(0, freq_devs - 1)], near_send)
+        arrived(plane_ref.at[pl.ds(0, blk_devs - 1)], plane_send)
+        for step in range(blk_devs - 1):
+            arrived(outgoing.at[step], send_sem.at[step])
+        arrived(outgoing.at[blk_devs - 1, pl.ds(0, freq_devs - 1)], send_sem.at[blk_devs - 1])
+    with jax.named_scope("recv_wait"):
+        arrived(recv_ref.at[pl.ds(0, n - 1)], recv_sem)
+
+
+def fill_table(band_ref, fir_ref, table, freq_count):
+    cols = table.shape[0] // 2
+    time_count = table.shape[1]
+    taps = fir_ref.shape[1]
     period = freq_count * time_count
+    quarter = period // 4
+    row = lax.broadcasted_iota(jnp.int32, (cols, taps), 0)
+    time = lax.broadcasted_iota(jnp.int32, (cols, taps), 1)
     low = band_ref[0]
     high = band_ref[1]
     numerator = low * freq_count + (high - low) * (row >> 1)
+
+    def cosine(turn):
+        return cos_turns((turn & (period - 1)).astype(jnp.float32) * (1.0 / period))
+
     turn = numerator * time
-
-    def cosine(shift):
-        return cos_turns(((turn + shift) & (period - 1)).astype(jnp.float32) * (1.0 / period))
-
-    quarter = period // 4
-    part = (row & 1) * quarter
-    cos_full = cosine(part)
-    sin_full = cosine(part + 3 * quarter)
-    head = turn[:, :taps]
+    cos_in = cosine(turn)
+    sin_in = cosine(turn + 3 * quarter)
+    step = numerator * taps
+    cos_step = cosine(step)
+    sin_step = cosine(step + 3 * quarter)
+    last = turn + numerator * (time_count - taps) + (row & 1) * quarter
+    cos_last = cosine(last)
+    sin_last = cosine(last + 3 * quarter)
     lag = lax.broadcasted_iota(jnp.int32, (taps, taps), 0)
     late = lax.broadcasted_iota(jnp.int32, (taps, taps), 1)
     kept = jnp.where(lag < taps - late, 1.0, 0.0).astype(jnp.float32)
     fir = fir_ref[...]
-    scale = 1.0 / math.sqrt(time_count)
-
-    def head_cos(shift):
-        return cos_turns(((head + shift) & (period - 1)).astype(jnp.float32) * (1.0 / period))
-
-    sum_cos = dot(head_cos(0) * fir, kept, precision=lax.Precision.HIGHEST) * scale
-    sum_sin = dot(head_cos(3 * quarter) * fir, kept, precision=lax.Precision.HIGHEST) * scale
-    body = time_count - taps
-    mixed = jnp.concatenate(
-        [
-            cos_full[:, :body] * sum_cos[:, :1] - sin_full[:, :body] * sum_sin[:, :1],
-            cos_full[:, body:] * sum_cos - sin_full[:, body:] * sum_sin,
-        ],
-        1,
-    )
-    mixed_high = mixed.astype(jnp.bfloat16)
-    mixed_low = mixed - mixed_high.astype(jnp.float32)
-    table[...] = (
-        jnp.concatenate([mixed_high.astype(jnp.float32), mixed_low], 0).T.astype(jnp.bfloat16)
-    )
-
-    def spectrum_of(rows):
-        both = dot(rows, table[...]).T
-        return both[:cols] + both[cols:]
-
-
-    def near_copy(f, slot):
-        return pltpu.make_async_remote_copy(
-            src_ref=near_out.at[f],
-            dst_ref=near_in.at[slot],
-            send_sem=near_send.at[f],
-            recv_sem=near_recv.at[slot],
-            device_id=(f, me_b),
-            device_id_type=MESH,
-        )
-
-    def plane_copy(offset, slot):
-        return pltpu.make_async_remote_copy(
-            src_ref=plane_out,
-            dst_ref=plane_ref.at[slot],
-            send_sem=plane_send.at[offset],
-            recv_sem=plane_recv.at[slot],
-            device_id=(me_f, flipped(me_b, offset, blk_devs)),
-            device_id_type=MESH,
-        )
-
-    own_plane = pltpu.make_async_copy(plane_out, plane_ref.at[me_b], plane_own)
-
-    def remote(step, f):
-        block = flipped(me_b, offsets[step], blk_devs)
-        return pltpu.make_async_remote_copy(
-            src_ref=outgoing.at[step, f],
-            dst_ref=recv_ref.at[me],
-            send_sem=send_sem.at[step * freq_devs + f],
-            recv_sem=recv_sem.at[me],
-            device_id=(f, block),
-            device_id_type=MESH,
-        )
-
-    own = pltpu.make_async_copy(outgoing.at[blk_devs - 1, me_f], recv_ref.at[me], own_sem)
-    for step in range(blk_devs):
-        chunk_copy(step).wait()
-        values = spectrum_of(
-            traces_buf[pl.ds(step * per, per)].reshape(width, time_count)
-        )
-        values = values.reshape(freq_devs, PARTS, width)
-        values = jnp.concatenate([values[:, :, :half], values[:, :, half:]], 1)
-        outgoing[step] = values.astype(jnp.bfloat16)
-        if step == 0:
-            pl.semaphore_wait(barrier, n - 1)
-        first = 0
-        if step == blk_devs - 1:
-            own.start()
-            first = 1
-
-        @pl.loop(first, freq_devs)
-        def _(d):
-            remote(step, lax.rem(me_f + d, freq_devs)).start()
-
-        if step == 0:
-            spot_copy().wait()
-            near = spectrum_of(spots_buf[...].reshape(spots * 16, time_count)).astype(jnp.bfloat16)
-            spot_row = lax.broadcasted_iota(jnp.int32, (spots * 16, near_lanes), 0)
-            spot_col = lax.broadcasted_iota(jnp.int32, (spots * 16, near_lanes), 1)
-            shift = lax.rem(me_f, packed) * spots
-            pick = jnp.where(spot_row == (spot_col - shift) * 16, 1.0, 0.0).astype(jnp.bfloat16)
-            at_spots = dot(near, pick).reshape(freq_devs, PARTS, near_lanes)
-            at_spots = jnp.concatenate([at_spots] * (near_rows // PARTS), 1)
-            line = lax.broadcasted_iota(jnp.int32, at_spots.shape, 1) // PARTS
-            near_out[...] = jnp.where(line == me_f // packed, at_spots, 0.0).astype(jnp.bfloat16)
-
-            @pl.loop(1, freq_devs)
-            def _(d):
-                near_copy(lax.rem(me_f + d, freq_devs), me_f).start()
-
-        if step == blk_devs - 2:
-            total = near_out[me_f].astype(jnp.float32)
-            for d in range(1, freq_devs):
-                source = lax.rem(me_f + d, freq_devs)
-                near_copy(source, source).wait_recv()
-                total = total + near_in[source].astype(jnp.float32)
-            plane_out[...] = total.astype(jnp.bfloat16)
-            own_plane.start()
-            for offset in range(1, blk_devs):
-                plane_copy(offset, me_b).start()
-
-    rows = recv_ref.shape[1]
-    fill_sort(sort_ref, rows)
-    own_plane.wait()
-    for offset in range(1, blk_devs):
-        plane_copy(offset, flipped(me_b, offset, blk_devs)).wait_recv()
-    small[2].wait()
-    fill_left(freq_devs, targets_ref, plane_ref, left_ref)
-    own.wait()
-
-    @pl.loop(1, freq_devs)
-    def _(d):
-        near_copy(lax.rem(me_f + d, freq_devs), me_f).wait_send()
-
-    for offset in range(1, blk_devs):
-        plane_copy(offset, me_b).wait_send()
-    for step in range(blk_devs):
-
-        @pl.loop(1 if step == blk_devs - 1 else 0, freq_devs)
-        def _(d):
-            remote(step, lax.rem(me_f + d, freq_devs)).wait_send()
-
-    @pl.loop(1, n)
-    def _(d):
-        source = lax.rem(me + d, n)
-        pltpu.make_async_remote_copy(
-            src_ref=outgoing.at[0, 0],
-            dst_ref=recv_ref.at[source],
-            send_sem=send_sem.at[0],
-            recv_sem=recv_sem.at[source],
-            device_id=(lax.rem(source, freq_devs), source // freq_devs),
-            device_id_type=MESH,
-        ).wait_recv()
+    weighted = jnp.concatenate([cos_in * fir, sin_in * fir], 0)
+    sums = dot(weighted, kept, precision=lax.Precision.HIGHEST) * (1.0 / math.sqrt(time_count))
+    sum_cos = sums[:cols]
+    sum_sin = sums[cols:]
+    odd = (row & 1) == 1
+    cos_own = jnp.where(odd, -sin_in, cos_in)
+    sin_own = jnp.where(odd, cos_in, sin_in)
+    all_cos = jnp.broadcast_to(sum_cos[:, :1], (cols, taps))
+    all_sin = jnp.broadcast_to(sum_sin[:, :1], (cols, taps))
+    value = cos_own * all_cos - sin_own * all_sin
+    other = sin_own * all_cos + cos_own * all_sin
+    tiles = time_count // taps
+    for tile in range(tiles):
+        if tile == tiles - 1:
+            value = cos_last * sum_cos - sin_last * sum_sin
+        value_high = value.astype(jnp.bfloat16)
+        value_low = (value - value_high.astype(jnp.float32)).astype(jnp.bfloat16)
+        table[pl.ds(0, cols), pl.ds(tile * taps, taps)] = value_high
+        table[pl.ds(cols, cols), pl.ds(tile * taps, taps)] = value_low
+        if tile < tiles - 2:
+            value, other = (
+                value * cos_step - other * sin_step,
+                other * cos_step + value * sin_step,
+            )
 
 
 def fill_sort(sort_ref, rows):
@@ -381,7 +379,7 @@
             pltpu.VMEM((1, count), jnp.int32),
             pltpu.VMEM((n, col_stride, time_count), jnp.bfloat16),
             pltpu.VMEM((n, 16, time_count), jnp.bfloat16),
-            pltpu.VMEM((time_count, 2 * cols), jnp.bfloat16),
+            pltpu.VMEM((2 * cols, time_count), jnp.bfloat16),
             pltpu.VMEM((blk_devs, freq_devs, ROWS, lanes), jnp.bfloat16),
             pltpu.VMEM((freq_devs, near_rows, near_lanes), jnp.bfloat16),
             pltpu.VMEM((freq_devs, near_rows, near_lanes), jnp.bfloat16),
@@ -390,14 +388,12 @@
             pltpu.SemaphoreType.DMA((3,)),
             pltpu.SemaphoreType.DMA((blk_devs,)),
             pltpu.SemaphoreType.DMA,
-            pltpu.SemaphoreType.DMA,
-            pltpu.SemaphoreType.DMA((n,)),
-            pltpu.SemaphoreType.DMA((n,)),
-            pltpu.SemaphoreType.DMA((freq_devs,)),
-            pltpu.SemaphoreType.DMA((freq_devs,)),
-            pltpu.SemaphoreType.DMA,
             pltpu.SemaphoreType.DMA((blk_devs,)),
-            pltpu.SemaphoreType.DMA((blk_devs,)),
+            pltpu.SemaphoreType.DMA,
+            pltpu.SemaphoreType.DMA,
+            pltpu.SemaphoreType.DMA,
+            pltpu.SemaphoreType.DMA,
+            pltpu.SemaphoreType.DMA,
         ],
         compiler_params=pltpu.CompilerParams(
             collective_id=0, has_side_effects=True, vmem_limit_bytes=VMEM_LIMIT

time: 27.4 us -> 24.2 us (0.88)
  Pallas kernels: 27.3 us -> 24.1 us
    pallas_call x1, Pallas kernels: 23.4 us -> 20.2 us  [per_device(): pl.pallas_call(functools.partial(send_kernel, freq_devs, blk_devs, col_st...]
where the time goes in v2:
time: 24.2 us; the launch traced here: 24.1 us
  Pallas kernels  24.1 us (100%)
    pallas_call x1, Pallas kernels, per_device(): pl.pallas_call(functools.partial(send_kernel, freq_devs, blk_devs, col_st...  20.2 us
    pallas_call x1, Pallas kernels, per_device(): pl.pallas_call(product_kernel, out_shape=jax.ShapeDtypeStruct((FREQ_DEV,...  3.85 us

profile of v2, /device:TPU:0, one launch (start us, length us, event | category | flops | bytes accessed | tf_op | source)
XLA Modules:
  0.0 24.1 jit_solution(4496365220706117632)
XLA Ops:
  0.0 20.2 %shard_map.46 = (bf16[32,16,512]{2,1,0:T(8,128)(2,1)S(1)}, bf16[4,512,64]{2,1,0:T(8,128)(2,1)S(1)}, bf16[512,512]{1,0:T(8,128)(2,1)S(1)}) custom-call(s32[2]{0:T(128)} %band_hbm.1, f32[1,128]{1,0:T(1,128)} %bitcast.5, s32[1,256]{1,0:T(1,128)} %bitcast.4, bf16[32,128,1024]{2,1,0:T(8,128)(2,1)} %bitcast.3), custom_call_target="tpu_custom_call" | custom-call | tf_op jit(solution)/shard_map/pallas_call | solution.py:367
  20.2 3.8 %shard_map.47 = f32[4,2,256,1024]{3,2,1,0:T(8,128)} custom-call(bf16[32,16,512]{2,1,0:T(8,128)(2,1)S(1)} %get-tuple-element.8.recv_ref, bf16[4,512,64]{2,1,0:T(8,128)(2,1)S(1)} %get-tuple-element.9.left_ref, bf16[512,512]{1,0:T(8,128)(2,1)S(1)} %get-tuple-element.10.sort_ref), custom_call_target="tpu_custom_call" | custom-call | tf_op jit(solution)/shard_map/pallas_call | solution.py:407

commit v3 on v2

--- a/solution.py
+++ b/solution.py
@@ -12,7 +12,9 @@
 PARTS = 2 * FREQ_DEV
 ROWS = 2 * PARTS
 VMEM_LIMIT = 40 * 2**20
+VMEM_LARGE = 54 * 2**20
 GROUP = 32
+UNROLL = True
 MESH = pl.DeviceIdType.MESH
 
 
@@ -44,6 +46,7 @@
     band_hbm, fir_hbm, targets_hbm, traces_ref, recv_ref, left_ref, sort_ref,
     band_ref, fir_ref, targets_ref,
     traces_buf, spots_buf, table, outgoing, near_out, near_in, plane_out, plane_ref,
+    choose, pick, inside, fold, signs,
     small_sem, chunk_sem, spot_sem, send_sem, recv_sem,
     near_send, near_recv, plane_send, plane_recv,
 ):
@@ -54,34 +57,43 @@
     spots, _, time_count = traces_buf.shape
     rec_count = spots * col_stride
     width = rec_count // blk_devs
-    half = width // 2
+    lanes = width // 4
     freq_count = FREQ_DEV * freq_devs
     cols = 2 * freq_count
     per = width // col_stride
     _, near_rows, near_lanes = near_out.shape
     packed = near_lanes // spots
 
-    crossing = list(range(blk_devs // 2, blk_devs))
-    offsets = crossing + list(range(blk_devs // 2 - 1, -1, -1))
+    side = blk_devs // 2
+    own_side = me_b // side
+    low = 1 - own_side
+    blocks = [low * side + lax.rem(low * me_b + step, side) for step in range(side)]
+    blocks += [own_side * side + lax.rem(me_b + 1 + step, side) for step in range(side)]
+    piece = per // 2
 
     def spot_copy():
         return pltpu.make_async_copy(
             traces_ref.at[:, pl.ds(0, 16), :], spots_buf, spot_sem
         )
 
-    def chunk_copy(step):
-        block = flipped(me_b, offsets[step], blk_devs)
+    def chunk_copy(step, part):
         return pltpu.make_async_copy(
-            traces_ref.at[pl.ds(block * per, per)],
-            traces_buf.at[pl.ds(step * per, per)],
-            chunk_sem.at[step],
+            traces_ref.at[pl.ds(blocks[step] * per + part * piece, piece)],
+            traces_buf.at[pl.ds(step * per + part * piece, piece)],
+            chunk_sem.at[step, part],
         )
 
-    def enter(d):
-        to = lax.rem(me + d, n)
-        pl.semaphore_signal(
-            barrier, inc=1, device_id=(lax.rem(to, freq_devs), to // freq_devs), device_id_type=MESH
-        )
+    def signal_block(offset):
+        block = flipped(me_b, offset, blk_devs)
+
+        @pl.loop(0 if offset else 1, freq_devs, unroll=UNROLL)
+        def _(d):
+            pl.semaphore_signal(
+                barrier,
+                inc=1,
+                device_id=(lax.rem(me_f + d, freq_devs), block),
+                device_id_type=MESH,
+            )
 
     def near_copy(f):
         return pltpu.make_async_remote_copy(
@@ -103,16 +115,20 @@
             device_id_type=MESH,
         )
 
-    def remote(step, f):
-        block = flipped(me_b, offsets[step], blk_devs)
-        return pltpu.make_async_remote_copy(
-            src_ref=outgoing.at[step, f],
-            dst_ref=recv_ref.at[me],
-            send_sem=send_sem.at[step],
-            recv_sem=recv_sem,
-            device_id=(f, block),
-            device_id_type=MESH,
-        )
+    def send(step, parts):
+        first = 1 if step == blk_devs - 1 else 0
+
+        @pl.loop(first, freq_devs, unroll=UNROLL)
+        def _(d):
+            f = lax.rem(me_f + d, freq_devs)
+            pltpu.make_async_remote_copy(
+                src_ref=outgoing.at[step, f, parts],
+                dst_ref=recv_ref.at[me, parts],
+                send_sem=send_sem.at[step],
+                recv_sem=recv_sem,
+                device_id=(f, blocks[step]),
+                device_id_type=MESH,
+            ).start()
 
     def arrived(ref, sem):
         pltpu.make_async_copy(ref, ref, sem).wait()
@@ -123,23 +139,43 @@
         pltpu.make_async_copy(targets_hbm, targets_ref, small_sem.at[2]),
     ]
     barrier = pltpu.get_barrier_semaphore()
+    small[0].start()
+    small[1].start()
+    chunk_copy(0, 0).start()
     with jax.named_scope("signals"):
-        small[0].start()
-        small[1].start()
-        spot_copy().start()
-        pl.loop(1, n)(enter)
-    for step in range(blk_devs):
-        chunk_copy(step).start()
-    small[2].start()
+        for offset in range(blk_devs):
+            signal_block(offset)
+    spot_copy().start()
     with jax.named_scope("small_wait"):
         small[0].wait()
         small[1].wait()
+    chunk_copy(0, 1).start()
     with jax.named_scope("table"):
         fill_table(band_ref, fir_ref, table, freq_count)
 
     def spectrum_of(rows):
         both = dot(table[...], rows, (((1,), (1,)), ((), ())))
         return both[:cols] + both[cols:]
+
+    def spectra(step, part):
+        with jax.named_scope(f"chunk{step}{part}"):
+            chunk_copy(step, part).wait()
+            rows = traces_buf[pl.ds(step * per + part * piece, piece)]
+            values = spectrum_of(rows.reshape(2 * lanes, time_count))
+            values = values.reshape(freq_devs, PARTS, 2 * lanes)
+            values = jnp.concatenate([values[:, :, :lanes], values[:, :, lanes:]], 1)
+            outgoing[step, :, part] = values.astype(jnp.bfloat16)
+
+    chunk_copy(1, 0).start()
+    small[2].start()
+    spectra(0, 0)
+    chunk_copy(1, 1).start()
+    for step in range(2, blk_devs):
+        chunk_copy(step, 0).start()
+        chunk_copy(step, 1).start()
+    with jax.named_scope("barrier"):
+        pl.semaphore_wait(barrier, n - 1)
+    send(0, pl.ds(0, 1))
 
     with jax.named_scope("spots"):
         spot_copy().wait()
@@ -147,28 +183,22 @@
         spot_row = lax.broadcasted_iota(jnp.int32, (spots * 16, near_lanes), 0)
         spot_col = lax.broadcasted_iota(jnp.int32, (spots * 16, near_lanes), 1)
         shift = lax.rem(me_f, packed) * spots
-        pick = jnp.where(spot_row == (spot_col - shift) * 16, 1.0, 0.0).astype(jnp.bfloat16)
-        at_spots = dot(near, pick).reshape(freq_devs, PARTS, near_lanes)
+        at_spot = jnp.where(spot_row == (spot_col - shift) * 16, 1.0, 0.0).astype(jnp.bfloat16)
+        at_spots = dot(near, at_spot).reshape(freq_devs, PARTS, near_lanes)
         at_spots = jnp.concatenate([at_spots] * (near_rows // PARTS), 1)
         line = lax.broadcasted_iota(jnp.int32, at_spots.shape, 1) // PARTS
         near_out[...] = jnp.where(line == me_f // packed, at_spots, 0.0).astype(jnp.bfloat16)
         near_in[me_f] = near_out[me_f]
 
-    for step in range(blk_devs):
-        with jax.named_scope(f"chunk{step}"):
-            chunk_copy(step).wait()
-            values = spectrum_of(traces_buf[pl.ds(step * per, per)].reshape(width, time_count))
-            values = values.reshape(freq_devs, PARTS, width)
-            values = jnp.concatenate([values[:, :, :half], values[:, :, half:]], 1)
-            outgoing[step] = values.astype(jnp.bfloat16)
-        if step == 0:
-            with jax.named_scope("barrier"):
-                pl.semaphore_wait(barrier, n - 1)
-
-            @pl.loop(1, freq_devs)
-            def _(d):
-                near_copy(lax.rem(me_f + d, freq_devs)).start()
-
+    @pl.loop(1, freq_devs, unroll=UNROLL)
+    def _(d):
+        near_copy(lax.rem(me_f + d, freq_devs)).start()
+
+    spectra(0, 1)
+    send(0, pl.ds(1, 1))
+    for step in range(1, blk_devs):
+        spectra(step, 0)
+        spectra(step, 1)
         if step == 1:
             with jax.named_scope("plane"):
                 arrived(near_in.at[pl.ds(0, freq_devs - 1)], near_recv)
@@ -177,25 +207,19 @@
                 plane_ref[me_b] = plane_out[...]
             for offset in range(1, blk_devs):
                 plane_copy(offset, me_b).start()
-
-        first = 0
         if step == blk_devs - 1:
             recv_ref[me] = outgoing[step, me_f]
-            first = 1
-
-        with jax.named_scope("send"):
-
-            @pl.loop(first, freq_devs)
-            def _(d):
-                remote(step, lax.rem(me_f + d, freq_devs)).start()
+        send(step, pl.ds(0, 2))
 
     with jax.named_scope("sort"):
-        fill_sort(sort_ref, recv_ref.shape[1])
+        fill_sort(sort_ref, recv_ref.shape[2])
+    with jax.named_scope("choice"):
+        small[2].wait()
+        fill_choice(freq_devs, packed, targets_ref, choose, pick, inside, fold, signs)
     with jax.named_scope("plane_wait"):
         arrived(plane_ref.at[pl.ds(0, blk_devs - 1)], plane_recv)
-        small[2].wait()
     with jax.named_scope("left"):
-        fill_left(freq_devs, targets_ref, plane_ref, left_ref)
+        fill_left(plane_ref, choose, pick, inside, fold, signs, left_ref)
     with jax.named_scope("send_wait"):
         arrived(near_in.at[pl.ds(0, freq_devs - 1)], near_send)
         arrived(plane_ref.at[pl.ds(0, blk_devs - 1)], plane_send)
@@ -270,51 +294,62 @@
     sort_ref[...] = jnp.where(place == home, 1.0, 0.0).astype(jnp.bfloat16)
 
 
-def fill_left(freq_devs, targets_ref, plane_ref, left_ref):
+def fill_choice(freq_devs, packed, targets_ref, choose, pick, inside, fold, signs):
+    count = targets_ref.shape[1]
+    shots = choose.shape[1] // 2
+    lines, depth = pick.shape
+    near_lanes, wide = fold.shape
+    near_rows = freq_devs // packed * PARTS
+    wanted = jnp.broadcast_to(targets_ref[...].astype(jnp.float32), (128, count)).T
+    shot = lax.broadcasted_iota(jnp.int32, (count, 2 * shots), 1) % shots
+    choose[...] = jnp.where(shot == wanted[:, :1].astype(jnp.int32), 1.0, 0.0).astype(jnp.bfloat16)
+
+    line = lax.broadcasted_iota(jnp.int32, (lines, depth), 0)
+    place = lax.broadcasted_iota(jnp.int32, (lines, depth), 1)
+    part = line // shots
+    from_shot = line % shots
+    from_f = from_shot % freq_devs
+    home = (from_shot // freq_devs) * near_rows + (from_f // packed) * PARTS + part
+    pick[...] = jnp.where(place == home, 1.0, 0.0).astype(jnp.bfloat16)
+
+    line = lax.broadcasted_iota(jnp.int32, (lines, near_lanes), 0)
+    lane = lax.broadcasted_iota(jnp.int32, (lines, near_lanes), 1)
+    slot = line % shots % freq_devs % packed
+    inside[...] = jnp.where(lane // shots == slot, 1.0, 0.0)
+
+    row = lax.broadcasted_iota(jnp.int32, (near_lanes, wide), 0)
+    lane = lax.broadcasted_iota(jnp.int32, (near_lanes, wide), 1)
+    spot = lane // (2 * GROUP) * GROUP + lane % GROUP
+    fold[...] = jnp.where(row % shots == spot % shots, 1.0, 0.0).astype(jnp.bfloat16)
+
+    source = lax.broadcasted_iota(jnp.int32, (2 * shots, wide), 0) // shots
+    lane = lax.broadcasted_iota(jnp.int32, (2 * shots, wide), 1)
+    target = lane // GROUP % 2
+    used = jnp.where(lane < 2 * shots, 1.0, 0.0)
+    signs[0] = jnp.where(source == target, jnp.where(source == 1, -used, used), 0.0)
+    signs[1] = jnp.where(source == target, 0.0, used)
+
+
+def fill_left(plane_ref, choose, pick, inside, fold, signs, left_ref):
     blk_devs, near_rows, near_lanes = plane_ref.shape
-    shots = left_ref.shape[2] // 2
-    packed = near_lanes // shots
-    count = targets_ref.shape[1]
-    wide = max(128, 2 * shots)
-    wanted = jnp.broadcast_to(targets_ref[...].astype(jnp.float32), (128, count)).T
-    shot = lax.broadcasted_iota(jnp.int32, (count, 2 * shots), 1)
-    shot = jnp.where(shot >= shots, shot - shots, shot)
-    chooser = jnp.where(shot == wanted[:, :1].astype(jnp.int32), 1.0, 0.0).astype(jnp.bfloat16)
-    fold_row = lax.broadcasted_iota(jnp.int32, (near_lanes, wide), 0)
-    fold_col = lax.broadcasted_iota(jnp.int32, (near_lanes, wide), 1)
-    fold_spot = fold_col // (2 * GROUP) * GROUP + fold_col % GROUP
-    fold = jnp.where(fold_row % shots == fold_spot % shots, 1.0, 0.0).astype(jnp.bfloat16)
-    near_depth = blk_devs * near_rows
+    count, depth = choose.shape
+    wide = fold.shape[1]
+    planes = plane_ref[...].reshape(blk_devs * near_rows, near_lanes)
+    near = (dot(pick[...], planes) * inside[...]).astype(jnp.bfloat16)
+    near = dot(near, fold[...])
+    parts = []
     for i in range(FREQ_DEV):
-        line = lax.broadcasted_iota(jnp.int32, (2 * shots, near_depth), 0)
-        place = lax.broadcasted_iota(jnp.int32, (2 * shots, near_depth), 1)
-        part = line // shots
-        from_shot = line - part * shots
-        from_f = from_shot % freq_devs
-        home = (from_shot // freq_devs) * near_rows + (from_f // packed) * PARTS + 2 * i + part
-        pick = jnp.where(place == home, 1.0, 0.0).astype(jnp.bfloat16)
-        near = dot(pick, plane_ref[...].reshape(near_depth, near_lanes))
-        slot = lax.broadcasted_iota(jnp.int32, near.shape, 0) % freq_devs % packed
-        lane = lax.broadcasted_iota(jnp.int32, near.shape, 1)
-        near = jnp.where(lane // shots == slot, near, 0.0).astype(jnp.bfloat16)
-        near = dot(near, fold)
-        source = lax.broadcasted_iota(jnp.int32, near.shape, 0) >= shots
-        lane = lax.broadcasted_iota(jnp.int32, near.shape, 1)
-        target = lane // GROUP % 2 == 1
-        inside = lane < 2 * shots
-        same = inside & (source == target)
-        other = inside & (source != target)
-        parts = [
-            jnp.where(same, jnp.where(source, -near, near), 0.0),
-            jnp.where(other, near, 0.0),
-        ]
         for o in range(2):
-            left = dot(chooser, parts[o].astype(jnp.bfloat16)).astype(jnp.bfloat16)
-            left_ref[i, pl.ds(o * count, count), :] = left[:, : 2 * shots]
+            parts.append((near[i * depth : (i + 1) * depth] * signs[o]).astype(jnp.bfloat16))
+    lefts = dot(choose[...], jnp.concatenate(parts, 1)).astype(jnp.bfloat16)
+    for i in range(FREQ_DEV):
+        for o in range(2):
+            k = 2 * i + o
+            left_ref[i, pl.ds(o * count, count), :] = lefts[:, k * wide : (k + 1) * wide]
 
 
 def product_kernel(recv_ref, left_ref, sort_ref, out_ref, made, sems):
-    shots, rows, half = recv_ref.shape
+    shots, pieces, rows, lanes = recv_ref.shape
     count = left_ref.shape[1] // 2
     span = GROUP * rows
     scale = 1.0 / math.sqrt(shots)
@@ -326,18 +361,19 @@
 
     for i in range(FREQ_DEV):
         lines = sort_ref[pl.ds(i * 4 * GROUP, 4 * GROUP), :]
-        rights = [
-            dot(lines, recv_ref[pl.ds(g * GROUP, GROUP)].reshape(span, half)).astype(jnp.bfloat16)
-            for g in range(shots // GROUP)
-        ]
-        rights = [
-            jnp.concatenate([r[2 * GROUP * h : 2 * GROUP * (h + 1)] for r in rights], 0)
-            for h in range(2)
-        ]
+        rights = []
+        for p in range(pieces):
+            sorted_rows = []
+            for g in range(shots // GROUP):
+                received = recv_ref[pl.ds(g * GROUP, GROUP), p].reshape(span, lanes)
+                sorted_rows.append(dot(lines, received).astype(jnp.bfloat16))
+            for h in range(2):
+                part = slice(2 * GROUP * h, 2 * GROUP * (h + 1))
+                rights.append(jnp.concatenate([r[part] for r in sorted_rows], 0))
         for o in range(2):
-            left = left_ref[i, pl.ds(o * count, count), :]
-            for h in range(2):
-                made[i, pl.ds(o * count, count), pl.ds(h * half, half)] = dot(left, rights[h]) * scale
+            left = left_ref[i, pl.ds(o * count, count), : 2 * shots]
+            for h, right in enumerate(rights):
+                made[i, pl.ds(o * count, count), pl.ds(h * lanes, lanes)] = dot(left, right) * scale
             write(i, o).start()
 
     for i in range(FREQ_DEV):
@@ -354,21 +390,22 @@
     assert blk_devs & (blk_devs - 1) == 0
     col_stride = rec_count // n
     width = rec_count // blk_devs
-    half = width // 2
-    lanes = half
+    lanes = width // 4
     near_lanes = max(128, n)
     packed = near_lanes // n
     near_rows = freq_devs // packed * PARTS
     cols = 2 * FREQ_DEV * freq_devs
     count = targets.shape[0]
     assert n % GROUP == 0
+    limit = VMEM_LIMIT if n <= 64 else VMEM_LARGE
     lines = 4 * FREQ_DEV * GROUP
+    wide = max(128, 2 * n)
     hbm = lambda x: pltpu.with_memory_space_constraint(x, pltpu.HBM)
     received, lefts, sorter = pl.pallas_call(
         functools.partial(send_kernel, freq_devs, blk_devs, col_stride),
         out_shape=[
-            pltpu.VMEM((n, ROWS, lanes), jnp.bfloat16),
-            pltpu.VMEM((FREQ_DEV, 2 * count, 2 * n), jnp.bfloat16),
+            pltpu.VMEM((n, 2, ROWS, lanes), jnp.bfloat16),
+            pltpu.VMEM((FREQ_DEV, 2 * count, wide), jnp.bfloat16),
             pltpu.VMEM((lines, GROUP * ROWS), jnp.bfloat16),
         ],
         in_specs=[pl.BlockSpec(memory_space=pl.ANY)] * 4,
@@ -380,13 +417,18 @@
             pltpu.VMEM((n, col_stride, time_count), jnp.bfloat16),
             pltpu.VMEM((n, 16, time_count), jnp.bfloat16),
             pltpu.VMEM((2 * cols, time_count), jnp.bfloat16),
-            pltpu.VMEM((blk_devs, freq_devs, ROWS, lanes), jnp.bfloat16),
+            pltpu.VMEM((blk_devs, freq_devs, 2, ROWS, lanes), jnp.bfloat16),
             pltpu.VMEM((freq_devs, near_rows, near_lanes), jnp.bfloat16),
             pltpu.VMEM((freq_devs, near_rows, near_lanes), jnp.bfloat16),
             pltpu.VMEM((near_rows, near_lanes), jnp.bfloat16),
             pltpu.VMEM((blk_devs, near_rows, near_lanes), jnp.bfloat16),
+            pltpu.VMEM((count, 2 * n), jnp.bfloat16),
+            pltpu.VMEM((FREQ_DEV * 2 * n, blk_devs * near_rows), jnp.bfloat16),
+            pltpu.VMEM((FREQ_DEV * 2 * n, near_lanes), jnp.float32),
+            pltpu.VMEM((near_lanes, wide), jnp.bfloat16),
+            pltpu.VMEM((2, 2 * n, wide), jnp.float32),
             pltpu.SemaphoreType.DMA((3,)),
-            pltpu.SemaphoreType.DMA((blk_devs,)),
+            pltpu.SemaphoreType.DMA((blk_devs, 2)),
             pltpu.SemaphoreType.DMA,
             pltpu.SemaphoreType.DMA((blk_devs,)),
             pltpu.SemaphoreType.DMA,
@@ -396,7 +438,7 @@
             pltpu.SemaphoreType.DMA,
         ],
         compiler_params=pltpu.CompilerParams(
-            collective_id=0, has_side_effects=True, vmem_limit_bytes=VMEM_LIMIT
+            collective_id=0, has_side_effects=True, vmem_limit_bytes=limit
         ),
     )(
         hbm(band),
@@ -413,7 +455,7 @@
             pltpu.VMEM((FREQ_DEV, 2 * count, width), jnp.float32),
             pltpu.SemaphoreType.DMA((FREQ_DEV, 2)),
         ],
-        compiler_params=pltpu.CompilerParams(vmem_limit_bytes=VMEM_LIMIT),
+        compiler_params=pltpu.CompilerParams(vmem_limit_bytes=limit),
     )(received, lefts, sorter)
 
 

time: 24.2 us -> 22 us (0.909)
  Pallas kernels: 24.1 us -> 21.8 us
    pallas_call x1, Pallas kernels: 20.2 us -> 18 us  [per_device(): pl.pallas_call(functools.partial(send_kernel, freq_devs, blk_devs, col_st...]
where the time goes in v3:
time: 22 us; the launch traced here: 21.8 us
  Pallas kernels  21.8 us (99%)
    pallas_call x1, Pallas kernels, per_device(): pl.pallas_call(functools.partial(send_kernel, freq_devs, blk_devs, col_st...  18 us
    pallas_call x1, Pallas kernels, per_device(): pl.pallas_call(product_kernel, out_shape=jax.ShapeDtypeStruct((FREQ_DEV,...  3.85 us

profile of v3, /device:TPU:0, one launch (start us, length us, event | category | flops | bytes accessed | tf_op | source)
XLA Modules:
  0.0 21.8 jit_solution(10295664049312445820)
XLA Ops:
  0.0 18.0 %shard_map.46 = (bf16[32,2,16,256]{3,2,1,0:T(8,128)(2,1)S(1)}, bf16[4,512,128]{2,1,0:T(8,128)(2,1)S(1)}, bf16[512,512]{1,0:T(8,128)(2,1)S(1)}) custom-call(s32[2]{0:T(128)} %band_hbm.1, f32[1,128]{1,0:T(1,128)} %bitcast.5, s32[1,256]{1,0:T(1,128)} %bitcast.4, bf16[32,128,1024]{2,1,0:T(8,128)(2,1)} %bitcast.3), custom_call_target="tpu_custom_call" | custom-call | tf_op jit(solution)/shard_map/pallas_call | solution.py:404
  18.0 3.9 %shard_map.47 = f32[4,2,256,1024]{3,2,1,0:T(8,128)} custom-call(bf16[32,2,16,256]{3,2,1,0:T(8,128)(2,1)S(1)} %get-tuple-element.8.recv_ref, bf16[4,512,128]{2,1,0:T(8,128)(2,1)S(1)} %get-tuple-element.9.left_ref, bf16[512,512]{1,0:T(8,128)(2,1)S(1)} %get-tuple-element.10.sort_ref), custom_call_target="tpu_custom_call" | custom-call | tf_op jit(solution)/shard_map/pallas_call | solution.py:449

commit v4 on v3

--- a/solution.py
+++ b/solution.py
@@ -12,7 +12,7 @@
 PARTS = 2 * FREQ_DEV
 ROWS = 2 * PARTS
 VMEM_LIMIT = 40 * 2**20
-VMEM_LARGE = 54 * 2**20
+VMEM_LARGE = 58 * 2**20
 GROUP = 32
 UNROLL = True
 MESH = pl.DeviceIdType.MESH
@@ -45,10 +45,10 @@
     freq_devs, blk_devs, col_stride,
     band_hbm, fir_hbm, targets_hbm, traces_ref, recv_ref, left_ref, sort_ref,
     band_ref, fir_ref, targets_ref,
-    traces_buf, spots_buf, table, outgoing, near_out, near_in, plane_out, plane_ref,
+    traces_buf, spots_buf, table, outgoing, relay, near_out, near_in, plane_out, plane_ref,
     choose, pick, inside, fold, signs,
     small_sem, chunk_sem, spot_sem, send_sem, recv_sem,
-    near_send, near_recv, plane_send, plane_recv,
+    near_send, near_recv, plane_send, plane_recv, relay_send, relay_recv, go,
 ):
     me_f = lax.axis_index("freq")
     me_b = lax.axis_index("blk")
@@ -65,10 +65,19 @@
     packed = near_lanes // spots
 
     side = blk_devs // 2
-    own_side = me_b // side
-    low = 1 - own_side
-    blocks = [low * side + lax.rem(low * me_b + step, side) for step in range(side)]
-    blocks += [own_side * side + lax.rem(me_b + 1 + step, side) for step in range(side)]
+    high = me_b // side
+    depth = (1 - high) * (side - 1 - me_b) + high * (me_b - side)
+    mate_b = blk_devs - 1 - me_b
+    mate = mate_b * freq_devs + me_f
+    inner = depth == 0
+    last = me_b == blk_devs - 1
+    ranks = [lax.rem(depth + step, side) for step in range(side)]
+    blocks = [(1 - high) * (side + r) + high * (side - 1 - r) for r in ranks]
+    blocks += [high * side + lax.rem(me_b + 1 + step, side) for step in range(side)]
+    late = (me_b // side)
+    delayed = blocks[1]
+    blocks[1] = (1 - late) * delayed + late * blocks[side]
+    blocks[side] = (1 - late) * blocks[side] + late * delayed
     piece = per // 2
 
     def spot_copy():
@@ -83,17 +92,29 @@
             chunk_sem.at[step, part],
         )
 
-    def signal_block(offset):
-        block = flipped(me_b, offset, blk_devs)
-
-        @pl.loop(0 if offset else 1, freq_devs, unroll=UNROLL)
+    def signal(f, block, sem):
+        pl.semaphore_signal(sem, inc=1, device_id=(f, block), device_id_type=MESH)
+
+    def signal_block(block, first):
+        @pl.loop(first, freq_devs, unroll=UNROLL)
         def _(d):
-            pl.semaphore_signal(
-                barrier,
-                inc=1,
-                device_id=(lax.rem(me_f + d, freq_devs), block),
-                device_id_type=MESH,
-            )
+            signal(lax.rem(me_f + d, freq_devs), block, barrier)
+
+    def announce():
+        @pl.when(inner)
+        def _():
+            signal(me_f, mate_b, barrier)
+
+        for block in range(blk_devs - 1, -1, -1):
+            if block not in (side - 1, side):
+
+                @pl.when(me_b == block)
+                def _():
+                    signal_block(block, 1)
+
+                @pl.when(me_b != block)
+                def _():
+                    signal_block(block, 0)
 
     def near_copy(f):
         return pltpu.make_async_remote_copy(
@@ -117,16 +138,44 @@
 
     def send(step, parts):
         first = 1 if step == blk_devs - 1 else 0
+        turn = me_f if first else me_f * jnp.minimum(blocks[step], 1)
 
         @pl.loop(first, freq_devs, unroll=UNROLL)
         def _(d):
-            f = lax.rem(me_f + d, freq_devs)
+            f = lax.rem(turn + d, freq_devs)
             pltpu.make_async_remote_copy(
                 src_ref=outgoing.at[step, f, parts],
                 dst_ref=recv_ref.at[me, parts],
                 send_sem=send_sem.at[step],
                 recv_sem=recv_sem,
                 device_id=(f, blocks[step]),
+                device_id_type=MESH,
+            ).start()
+
+    def relay_copy(part):
+        return pltpu.make_async_remote_copy(
+            src_ref=outgoing.at[0, :, pl.ds(part, 1)],
+            dst_ref=relay.at[:, pl.ds(part, 1)],
+            send_sem=send_sem.at[0],
+            recv_sem=relay_recv.at[part],
+            device_id=(me_f, mate_b),
+            device_id_type=MESH,
+        )
+
+    def forward():
+        for part in range(2):
+            relay_copy(part).wait_recv()
+        recv_ref[mate] = relay[me_f]
+
+        @pl.loop(1, freq_devs, unroll=UNROLL)
+        def _(d):
+            f = lax.rem(me_f + d, freq_devs)
+            pltpu.make_async_remote_copy(
+                src_ref=relay.at[f],
+                dst_ref=recv_ref.at[mate],
+                send_sem=relay_send,
+                recv_sem=recv_sem,
+                device_id=(f, me_b),
                 device_id_type=MESH,
             ).start()
 
@@ -143,8 +192,7 @@
     small[1].start()
     chunk_copy(0, 0).start()
     with jax.named_scope("signals"):
-        for offset in range(blk_devs):
-            signal_block(offset)
+        announce()
     spot_copy().start()
     with jax.named_scope("small_wait"):
         small[0].wait()
@@ -168,14 +216,32 @@
 
     chunk_copy(1, 0).start()
     small[2].start()
-    spectra(0, 0)
-    chunk_copy(1, 1).start()
-    for step in range(2, blk_devs):
-        chunk_copy(step, 0).start()
-        chunk_copy(step, 1).start()
-    with jax.named_scope("barrier"):
-        pl.semaphore_wait(barrier, n - 1)
-    send(0, pl.ds(0, 1))
+    @pl.when(last)
+    def _():
+        with jax.named_scope("barrier"):
+            pl.semaphore_wait(barrier, n - 1)
+        signal(me_f, side, go)
+        signal(me_f, side - 1, go)
+
+    for part in range(2):
+        spectra(0, part)
+
+        @pl.when(inner)
+        def _():
+            if part == 0:
+                with jax.named_scope("mate"):
+                    pl.semaphore_wait(barrier, 1)
+            relay_copy(part).start()
+
+        @pl.when(last)
+        def _():
+            send(0, pl.ds(part, 1))
+
+        if part == 0:
+            chunk_copy(1, 1).start()
+            for step in range(2, blk_devs):
+                chunk_copy(step, 0).start()
+                chunk_copy(step, 1).start()
 
     with jax.named_scope("spots"):
         spot_copy().wait()
@@ -190,23 +256,43 @@
         near_out[...] = jnp.where(line == me_f // packed, at_spots, 0.0).astype(jnp.bfloat16)
         near_in[me_f] = near_out[me_f]
 
+    @pl.when(inner)
+    def _():
+        with jax.named_scope("go"):
+            pl.semaphore_wait(go, 1)
+
+    outer_rest = jnp.logical_not(jnp.logical_or(inner, last))
+
+    @pl.when(outer_rest)
+    def _():
+        with jax.named_scope("barrier"):
+            pl.semaphore_wait(barrier, n - 1)
+
     @pl.loop(1, freq_devs, unroll=UNROLL)
     def _(d):
         near_copy(lax.rem(me_f + d, freq_devs)).start()
 
-    spectra(0, 1)
-    send(0, pl.ds(1, 1))
-    for step in range(1, blk_devs):
+    @pl.when(outer_rest)
+    def _():
+        send(0, pl.ds(0, 2))
+
+    spectra(1, 0)
+    send(1, pl.ds(0, 1))
+    spectra(1, 1)
+    spectra(2, 0)
+    spectra(2, 1)
+    with jax.named_scope("plane"):
+        arrived(near_in.at[pl.ds(0, freq_devs - 1)], near_recv)
+        total = near_in[...].astype(jnp.float32)
+        plane_out[...] = jnp.sum(total, 0).astype(jnp.bfloat16)
+        plane_ref[me_b] = plane_out[...]
+    for offset in range(1, blk_devs):
+        plane_copy(offset, me_b).start()
+    send(1, pl.ds(1, 1))
+    send(2, pl.ds(0, 2))
+    for step in range(3, blk_devs):
         spectra(step, 0)
         spectra(step, 1)
-        if step == 1:
-            with jax.named_scope("plane"):
-                arrived(near_in.at[pl.ds(0, freq_devs - 1)], near_recv)
-                total = near_in[...].astype(jnp.float32)
-                plane_out[...] = jnp.sum(total, 0).astype(jnp.bfloat16)
-                plane_ref[me_b] = plane_out[...]
-            for offset in range(1, blk_devs):
-                plane_copy(offset, me_b).start()
         if step == blk_devs - 1:
             recv_ref[me] = outgoing[step, me_f]
         send(step, pl.ds(0, 2))
@@ -216,6 +302,12 @@
     with jax.named_scope("choice"):
         small[2].wait()
         fill_choice(freq_devs, packed, targets_ref, choose, pick, inside, fold, signs)
+
+    @pl.when(inner)
+    def _():
+        with jax.named_scope("forward"):
+            forward()
+
     with jax.named_scope("plane_wait"):
         arrived(plane_ref.at[pl.ds(0, blk_devs - 1)], plane_recv)
     with jax.named_scope("left"):
@@ -227,7 +319,15 @@
             arrived(outgoing.at[step], send_sem.at[step])
         arrived(outgoing.at[blk_devs - 1, pl.ds(0, freq_devs - 1)], send_sem.at[blk_devs - 1])
     with jax.named_scope("recv_wait"):
-        arrived(recv_ref.at[pl.ds(0, n - 1)], recv_sem)
+
+        @pl.when(inner)
+        def _():
+            arrived(relay.at[pl.ds(0, freq_devs - 1)], relay_send)
+            arrived(recv_ref.at[pl.ds(0, n - 2)], recv_sem)
+
+        @pl.when(jnp.logical_not(inner))
+        def _():
+            arrived(recv_ref.at[pl.ds(0, n - 1)], recv_sem)
 
 
 def fill_table(band_ref, fir_ref, table, freq_count):
@@ -418,6 +518,7 @@
             pltpu.VMEM((n, 16, time_count), jnp.bfloat16),
             pltpu.VMEM((2 * cols, time_count), jnp.bfloat16),
             pltpu.VMEM((blk_devs, freq_devs, 2, ROWS, lanes), jnp.bfloat16),
+            pltpu.VMEM((freq_devs, 2, ROWS, lanes), jnp.bfloat16),
             pltpu.VMEM((freq_devs, near_rows, near_lanes), jnp.bfloat16),
             pltpu.VMEM((freq_devs, near_rows, near_lanes), jnp.bfloat16),
             pltpu.VMEM((near_rows, near_lanes), jnp.bfloat16),
@@ -436,6 +537,9 @@
             pltpu.SemaphoreType.DMA,
             pltpu.SemaphoreType.DMA,
             pltpu.SemaphoreType.DMA,
+            pltpu.SemaphoreType.DMA,
+            pltpu.SemaphoreType.DMA((2,)),
+            pltpu.SemaphoreType.REGULAR,
         ],
         compiler_params=pltpu.CompilerParams(
             collective_id=0, has_side_effects=True, vmem_limit_bytes=limit

time: 22 us -> 21.6 us (0.982)
  the two profiles are of different devices: /device:TPU:0 before, /device:TPU:5 now
where the time goes in v4:
time: 21.6 us; the launch traced here: 21.5 us
  Pallas kernels  21.4 us (99%)
    pallas_call x1, Pallas kernels, per_device(): pl.pallas_call(functools.partial(send_kernel, freq_devs, blk_devs, col_st...  17.6 us
    pallas_call x1, Pallas kernels, per_device(): pl.pallas_call(product_kernel, out_shape=jax.ShapeDtypeStruct((FREQ_DEV,...  3.85 us

profile of v4, /device:TPU:5, one launch (start us, length us, event | category | flops | bytes accessed | tf_op | source)
XLA Modules:
  0.0 21.5 jit_solution(84388442187782687)
XLA Ops:
  0.0 17.6 %shard_map.46 = (bf16[32,2,16,256]{3,2,1,0:T(8,128)(2,1)S(1)}, bf16[4,512,128]{2,1,0:T(8,128)(2,1)S(1)}, bf16[512,512]{1,0:T(8,128)(2,1)S(1)}) custom-call(s32[2]{0:T(128)} %band_hbm.1, f32[1,128]{1,0:T(1,128)} %bitcast.5, s32[1,256]{1,0:T(1,128)} %bitcast.4, bf16[32,128,1024]{2,1,0:T(8,128)(2,1)} %bitcast.3), custom_call_target="tpu_custom_call" | custom-call | tf_op jit(solution)/shard_map/pallas_call | solution.py:504
  17.6 3.9 %shard_map.47 = f32[4,2,256,1024]{3,2,1,0:T(8,128)} custom-call(bf16[32,2,16,256]{3,2,1,0:T(8,128)(2,1)S(1)} %get-tuple-element.8.recv_ref, bf16[4,512,128]{2,1,0:T(8,128)(2,1)S(1)} %get-tuple-element.9.left_ref, bf16[512,512]{1,0:T(8,128)(2,1)S(1)} %get-tuple-element.10.sort_ref), custom_call_target="tpu_custom_call" | custom-call | tf_op jit(solution)/shard_map/pallas_call | solution.py:553

commit v5 on v4

--- a/solution.py
+++ b/solution.py
@@ -12,7 +12,7 @@
 PARTS = 2 * FREQ_DEV
 ROWS = 2 * PARTS
 VMEM_LIMIT = 40 * 2**20
-VMEM_LARGE = 58 * 2**20
+VMEM_LARGE = 52 * 2**20
 GROUP = 32
 UNROLL = True
 MESH = pl.DeviceIdType.MESH
@@ -43,7 +43,7 @@
 
 def send_kernel(
     freq_devs, blk_devs, col_stride,
-    band_hbm, fir_hbm, targets_hbm, traces_ref, recv_ref, left_ref, sort_ref,
+    band_hbm, fir_hbm, targets_hbm, traces_ref, recv_ref, left_ref, sort_ref, early_ref,
     band_ref, fir_ref, targets_ref,
     traces_buf, spots_buf, table, outgoing, relay, near_out, near_in, plane_out, plane_ref,
     choose, pick, inside, fold, signs,
@@ -136,18 +136,20 @@
             device_id_type=MESH,
         )
 
-    def send(step, parts):
+    def send(step, part, some=None):
         first = 1 if step == blk_devs - 1 else 0
         turn = me_f if first else me_f * jnp.minimum(blocks[step], 1)
 
-        @pl.loop(first, freq_devs, unroll=UNROLL)
+        start, stop = some or (first, freq_devs)
+
+        @pl.loop(start, stop, unroll=UNROLL)
         def _(d):
             f = lax.rem(turn + d, freq_devs)
             pltpu.make_async_remote_copy(
-                src_ref=outgoing.at[step, f, parts],
-                dst_ref=recv_ref.at[me, parts],
+                src_ref=outgoing.at[step, f, part],
+                dst_ref=recv_ref.at[me, part],
                 send_sem=send_sem.at[step],
-                recv_sem=recv_sem,
+                recv_sem=recv_sem.at[part],
                 device_id=(f, blocks[step]),
                 device_id_type=MESH,
             ).start()
@@ -162,22 +164,30 @@
             device_id_type=MESH,
         )
 
-    def forward():
-        for part in range(2):
-            relay_copy(part).wait_recv()
-        recv_ref[mate] = relay[me_f]
+    def forward(part):
+        relay_copy(part).wait_recv()
+        recv_ref[mate, part] = relay[me_f, part]
 
         @pl.loop(1, freq_devs, unroll=UNROLL)
         def _(d):
             f = lax.rem(me_f + d, freq_devs)
             pltpu.make_async_remote_copy(
-                src_ref=relay.at[f],
-                dst_ref=recv_ref.at[mate],
+                src_ref=relay.at[f, part],
+                dst_ref=recv_ref.at[mate, part],
                 send_sem=relay_send,
-                recv_sem=recv_sem,
+                recv_sem=recv_sem.at[part],
                 device_id=(f, me_b),
                 device_id_type=MESH,
             ).start()
+
+    def wait_part(part):
+        @pl.when(inner)
+        def _():
+            arrived(recv_ref.at[pl.ds(0, n - 2), part], recv_sem.at[part])
+
+        @pl.when(jnp.logical_not(inner))
+        def _():
+            arrived(recv_ref.at[pl.ds(0, n - 1), part], recv_sem.at[part])
 
     def arrived(ref, sem):
         pltpu.make_async_copy(ref, ref, sem).wait()
@@ -216,12 +226,42 @@
 
     chunk_copy(1, 0).start()
     small[2].start()
+    def spots_near():
+        with jax.named_scope("spots"):
+            spot_copy().wait()
+            shift = lax.rem(me_f, packed) * spots
+            taken = min(spots, 64)
+            at_spots = None
+            for first in range(0, spots, taken):
+                rows = spots_buf[pl.ds(first, taken)].reshape(taken * 16, time_count)
+                near = spectrum_of(rows).astype(jnp.bfloat16)
+                spot_row = lax.broadcasted_iota(jnp.int32, (taken * 16, near_lanes), 0)
+                spot_col = lax.broadcasted_iota(jnp.int32, (taken * 16, near_lanes), 1)
+                here = spot_row == (spot_col - shift - first) * 16
+                some = dot(near, jnp.where(here, 1.0, 0.0).astype(jnp.bfloat16))
+                at_spots = some if at_spots is None else at_spots + some
+            at_spots = at_spots.reshape(freq_devs, PARTS, near_lanes)
+            at_spots = jnp.concatenate([at_spots] * 2, 1)
+            line = lax.broadcasted_iota(jnp.int32, at_spots.shape, 1) // PARTS
+            for pair in range(near_rows // (2 * PARTS)):
+                kept = jnp.where(line + 2 * pair == me_f // packed, at_spots, 0.0)
+                near_out[:, pl.ds(2 * PARTS * pair, 2 * PARTS), :] = kept.astype(jnp.bfloat16)
+            near_in[me_f] = near_out[me_f]
+
+    def send_near():
+
+        @pl.loop(1, freq_devs, unroll=UNROLL)
+        def _(d):
+            near_copy(lax.rem(me_f + d, freq_devs)).start()
+
     @pl.when(last)
     def _():
         with jax.named_scope("barrier"):
             pl.semaphore_wait(barrier, n - 1)
         signal(me_f, side, go)
         signal(me_f, side - 1, go)
+        spots_near()
+        send_near()
 
     for part in range(2):
         spectra(0, part)
@@ -235,7 +275,7 @@
 
         @pl.when(last)
         def _():
-            send(0, pl.ds(part, 1))
+            send(0, part)
 
         if part == 0:
             chunk_copy(1, 1).start()
@@ -243,91 +283,154 @@
                 chunk_copy(step, 0).start()
                 chunk_copy(step, 1).start()
 
-    with jax.named_scope("spots"):
-        spot_copy().wait()
-        near = spectrum_of(spots_buf[...].reshape(spots * 16, time_count)).astype(jnp.bfloat16)
-        spot_row = lax.broadcasted_iota(jnp.int32, (spots * 16, near_lanes), 0)
-        spot_col = lax.broadcasted_iota(jnp.int32, (spots * 16, near_lanes), 1)
-        shift = lax.rem(me_f, packed) * spots
-        at_spot = jnp.where(spot_row == (spot_col - shift) * 16, 1.0, 0.0).astype(jnp.bfloat16)
-        at_spots = dot(near, at_spot).reshape(freq_devs, PARTS, near_lanes)
-        at_spots = jnp.concatenate([at_spots] * (near_rows // PARTS), 1)
-        line = lax.broadcasted_iota(jnp.int32, at_spots.shape, 1) // PARTS
-        near_out[...] = jnp.where(line == me_f // packed, at_spots, 0.0).astype(jnp.bfloat16)
-        near_in[me_f] = near_out[me_f]
+    outer_rest = jnp.logical_not(jnp.logical_or(inner, last))
+
+    @pl.when(jnp.logical_not(last))
+    def _():
+        spots_near()
 
     @pl.when(inner)
     def _():
         with jax.named_scope("go"):
             pl.semaphore_wait(go, 1)
 
-    outer_rest = jnp.logical_not(jnp.logical_or(inner, last))
-
     @pl.when(outer_rest)
     def _():
         with jax.named_scope("barrier"):
             pl.semaphore_wait(barrier, n - 1)
 
-    @pl.loop(1, freq_devs, unroll=UNROLL)
-    def _(d):
-        near_copy(lax.rem(me_f + d, freq_devs)).start()
+    @pl.when(jnp.logical_not(last))
+    def _():
+        send_near()
 
     @pl.when(outer_rest)
     def _():
-        send(0, pl.ds(0, 2))
-
+        send(0, 0)
+        send(0, 1)
+
+    tail = blk_devs - 1
     spectra(1, 0)
-    send(1, pl.ds(0, 1))
+    send(1, 0)
+    spectra(2, 0)
+    spectra(tail, 0)
     spectra(1, 1)
-    spectra(2, 0)
     spectra(2, 1)
     with jax.named_scope("plane"):
         arrived(near_in.at[pl.ds(0, freq_devs - 1)], near_recv)
-        total = near_in[...].astype(jnp.float32)
-        plane_out[...] = jnp.sum(total, 0).astype(jnp.bfloat16)
+        total = near_in[0].astype(jnp.float32)
+        for f in range(1, freq_devs):
+            total = total + near_in[f].astype(jnp.float32)
+        plane_out[...] = total.astype(jnp.bfloat16)
         plane_ref[me_b] = plane_out[...]
     for offset in range(1, blk_devs):
         plane_copy(offset, me_b).start()
-    send(1, pl.ds(1, 1))
-    send(2, pl.ds(0, 2))
-    for step in range(3, blk_devs):
-        spectra(step, 0)
-        spectra(step, 1)
-        if step == blk_devs - 1:
-            recv_ref[me] = outgoing[step, me_f]
-        send(step, pl.ds(0, 2))
-
+    recv_ref[me, 0] = outgoing[tail, me_f, 0]
+
+    @pl.when(me_b < side)
+    def _():
+        send(tail, 0)
+        send(2, 0)
+        send(1, 1)
+        send(2, 1)
+
+
+    @pl.when(me_b == side)
+    def _():
+        send(2, 0, (0, 2))
+        send(2, 1, (0, 2))
+        send(2, 0, (2, freq_devs))
+        send(2, 1, (2, freq_devs))
+        send(tail, 0)
+        send(1, 1)
+
+
+    @pl.when(last)
+    def _():
+        send(tail, 0)
+        send(1, 1)
+        send(2, 0)
+
+    for step in range(3, tail):
+        for part in range(2):
+            spectra(step, part)
+            send(step, part)
+    spectra(tail, 1)
+    recv_ref[me, 1] = outgoing[tail, me_f, 1]
+    send(tail, 1)
     with jax.named_scope("sort"):
         fill_sort(sort_ref, recv_ref.shape[2])
     with jax.named_scope("choice"):
         small[2].wait()
         fill_choice(freq_devs, packed, targets_ref, choose, pick, inside, fold, signs)
 
+    @pl.when(last)
+    def _():
+        arrived(outgoing.at[0], send_sem.at[0])
+        arrived(outgoing.at[1], send_sem.at[1])
+        arrived(outgoing.at[2, :, 0], send_sem.at[2])
+        send(2, 1)
+
+
     @pl.when(inner)
     def _():
         with jax.named_scope("forward"):
-            forward()
+            forward(0)
+            forward(1)
 
     with jax.named_scope("plane_wait"):
         arrived(plane_ref.at[pl.ds(0, blk_devs - 1)], plane_recv)
     with jax.named_scope("left"):
         fill_left(plane_ref, choose, pick, inside, fold, signs, left_ref)
+    with jax.named_scope("first_part"):
+        wait_part(0)
+    with jax.named_scope("product"):
+        for i in range(FREQ_DEV):
+            rights = sorted_part(sort_ref, recv_ref, i, 0)
+            for o in range(2):
+                product(left_ref, rights, i, o, early_ref)
     with jax.named_scope("send_wait"):
         arrived(near_in.at[pl.ds(0, freq_devs - 1)], near_send)
         arrived(plane_ref.at[pl.ds(0, blk_devs - 1)], plane_send)
-        for step in range(blk_devs - 1):
+
+        @pl.when(jnp.logical_not(last))
+        def _():
+            for step in range(3):
+                arrived(outgoing.at[step], send_sem.at[step])
+
+        @pl.when(last)
+        def _():
+            arrived(outgoing.at[2, :, 1], send_sem.at[2])
+
+        for step in range(3, blk_devs - 1):
             arrived(outgoing.at[step], send_sem.at[step])
         arrived(outgoing.at[blk_devs - 1, pl.ds(0, freq_devs - 1)], send_sem.at[blk_devs - 1])
+
+        @pl.when(inner)
+        def _():
+            arrived(relay.at[pl.ds(0, freq_devs - 1)], relay_send)
+
     with jax.named_scope("recv_wait"):
-
-        @pl.when(inner)
-        def _():
-            arrived(relay.at[pl.ds(0, freq_devs - 1)], relay_send)
-            arrived(recv_ref.at[pl.ds(0, n - 2)], recv_sem)
-
-        @pl.when(jnp.logical_not(inner))
-        def _():
-            arrived(recv_ref.at[pl.ds(0, n - 1)], recv_sem)
+        wait_part(1)
+
+
+def sorted_part(sort_ref, recv_ref, i, part):
+    shots, _, rows, lanes = recv_ref.shape
+    lines = sort_ref[pl.ds(i * 4 * GROUP, 4 * GROUP), :]
+    groups = []
+    for g in range(shots // GROUP):
+        received = recv_ref[pl.ds(g * GROUP, GROUP), part].reshape(GROUP * rows, lanes)
+        groups.append(dot(lines, received).astype(jnp.bfloat16))
+    halves = [slice(2 * GROUP * h, 2 * GROUP * (h + 1)) for h in range(2)]
+    return [jnp.concatenate([r[half] for r in groups], 0) for half in halves]
+
+
+def product(left_ref, rights, i, o, out_ref):
+    count = left_ref.shape[1] // 2
+    depth, lanes = rights[0].shape
+    scale = 1.0 / math.sqrt(depth // 2)
+    left = left_ref[i, pl.ds(o * count, count), :depth]
+    for h, right in enumerate(rights):
+        out_ref[i, pl.ds(o * count, count), pl.ds(h * lanes, lanes)] = dot(left, right) * scale
 
 
 def fill_table(band_ref, fir_ref, table, freq_count):
@@ -404,13 +507,15 @@
     shot = lax.broadcasted_iota(jnp.int32, (count, 2 * shots), 1) % shots
     choose[...] = jnp.where(shot == wanted[:, :1].astype(jnp.int32), 1.0, 0.0).astype(jnp.bfloat16)
 
-    line = lax.broadcasted_iota(jnp.int32, (lines, depth), 0)
-    place = lax.broadcasted_iota(jnp.int32, (lines, depth), 1)
-    part = line // shots
-    from_shot = line % shots
-    from_f = from_shot % freq_devs
-    home = (from_shot // freq_devs) * near_rows + (from_f // packed) * PARTS + part
-    pick[...] = jnp.where(place == home, 1.0, 0.0).astype(jnp.bfloat16)
+    taken = lines if shots <= 64 else shots
+    for first in range(0, lines, taken):
+        line = lax.broadcasted_iota(jnp.int32, (taken, depth), 0) + first
+        place = lax.broadcasted_iota(jnp.int32, (taken, depth), 1)
+        part = line // shots
+        from_shot = line % shots
+        from_f = from_shot % freq_devs
+        home = (from_shot // freq_devs) * near_rows + (from_f // packed) * PARTS + part
+        pick[pl.ds(first, taken), :] = jnp.where(place == home, 1.0, 0.0).astype(jnp.bfloat16)
 
     line = lax.broadcasted_iota(jnp.int32, (lines, near_lanes), 0)
     lane = lax.broadcasted_iota(jnp.int32, (lines, near_lanes), 1)
@@ -434,51 +539,47 @@
     blk_devs, near_rows, near_lanes = plane_ref.shape
     count, depth = choose.shape
     wide = fold.shape[1]
+    batch = FREQ_DEV if depth <= 128 else 1
     planes = plane_ref[...].reshape(blk_devs * near_rows, near_lanes)
-    near = (dot(pick[...], planes) * inside[...]).astype(jnp.bfloat16)
-    near = dot(near, fold[...])
-    parts = []
+    for first in range(0, FREQ_DEV, batch):
+        lines = pl.ds(first * depth, batch * depth)
+        near = (dot(pick[lines, :], planes) * inside[lines, :]).astype(jnp.bfloat16)
+        near = dot(near, fold[...])
+        parts = []
+        for i in range(batch):
+            for o in range(2):
+                parts.append((near[i * depth : (i + 1) * depth] * signs[o]).astype(jnp.bfloat16))
+        lefts = dot(choose[...], jnp.concatenate(parts, 1)).astype(jnp.bfloat16)
+        for k in range(2 * batch):
+            o = k % 2
+            rows = pl.ds(o * count, count)
+            left_ref[first + k // 2, rows, :] = lefts[:, k * wide : (k + 1) * wide]
+
+
+def product_kernel(early_ref, recv_ref, left_ref, sort_ref, out_ref, made, sems):
+    half = made.shape[2]
+    count = made.shape[1] // 2
+
+    def write(source, i, o, part):
+        return pltpu.make_async_copy(
+            source.at[i, pl.ds(o * count, count)],
+            out_ref.at[i, o, :, pl.ds(part * half, half)],
+            sems.at[part, i, o],
+        )
+
     for i in range(FREQ_DEV):
         for o in range(2):
-            parts.append((near[i * depth : (i + 1) * depth] * signs[o]).astype(jnp.bfloat16))
-    lefts = dot(choose[...], jnp.concatenate(parts, 1)).astype(jnp.bfloat16)
+            write(early_ref, i, o, 0).start()
     for i in range(FREQ_DEV):
+        rights = sorted_part(sort_ref, recv_ref, i, 1)
         for o in range(2):
-            k = 2 * i + o
-            left_ref[i, pl.ds(o * count, count), :] = lefts[:, k * wide : (k + 1) * wide]
-
-
-def product_kernel(recv_ref, left_ref, sort_ref, out_ref, made, sems):
-    shots, pieces, rows, lanes = recv_ref.shape
-    count = left_ref.shape[1] // 2
-    span = GROUP * rows
-    scale = 1.0 / math.sqrt(shots)
-
-    def write(i, o):
-        return pltpu.make_async_copy(
-            made.at[i, pl.ds(o * count, count)], out_ref.at[i, o], sems.at[i, o]
-        )
-
-    for i in range(FREQ_DEV):
-        lines = sort_ref[pl.ds(i * 4 * GROUP, 4 * GROUP), :]
-        rights = []
-        for p in range(pieces):
-            sorted_rows = []
-            for g in range(shots // GROUP):
-                received = recv_ref[pl.ds(g * GROUP, GROUP), p].reshape(span, lanes)
-                sorted_rows.append(dot(lines, received).astype(jnp.bfloat16))
-            for h in range(2):
-                part = slice(2 * GROUP * h, 2 * GROUP * (h + 1))
-                rights.append(jnp.concatenate([r[part] for r in sorted_rows], 0))
-        for o in range(2):
-            left = left_ref[i, pl.ds(o * count, count), : 2 * shots]
-            for h, right in enumerate(rights):
-                made[i, pl.ds(o * count, count), pl.ds(h * lanes, lanes)] = dot(left, right) * scale
-            write(i, o).start()
-
-    for i in range(FREQ_DEV):
-        for o in range(2):
-            write(i, o).wait()
+            product(left_ref, rights, i, o, made)
+            write(made, i, o, 1).start()
+
+    for part, source in enumerate((early_ref, made)):
+        for i in range(FREQ_DEV):
+            for o in range(2):
+                write(source, i, o, part).wait()
 
 
 def per_device(traces, fir, targets, band):
@@ -501,15 +602,16 @@
     lines = 4 * FREQ_DEV * GROUP
     wide = max(128, 2 * n)
     hbm = lambda x: pltpu.with_memory_space_constraint(x, pltpu.HBM)
-    received, lefts, sorter = pl.pallas_call(
+    received, lefts, sorter, early = pl.pallas_call(
         functools.partial(send_kernel, freq_devs, blk_devs, col_stride),
         out_shape=[
             pltpu.VMEM((n, 2, ROWS, lanes), jnp.bfloat16),
             pltpu.VMEM((FREQ_DEV, 2 * count, wide), jnp.bfloat16),
             pltpu.VMEM((lines, GROUP * ROWS), jnp.bfloat16),
+            pltpu.VMEM((FREQ_DEV, 2 * count, width // 2), jnp.float32),
         ],
         in_specs=[pl.BlockSpec(memory_space=pl.ANY)] * 4,
-        out_specs=[pl.BlockSpec(memory_space=pltpu.VMEM)] * 3,
+        out_specs=[pl.BlockSpec(memory_space=pltpu.VMEM)] * 4,
         scratch_shapes=[
             pltpu.SMEM((2,), jnp.int32),
             pltpu.VMEM((1, fir.shape[0]), jnp.float32),
@@ -532,7 +634,7 @@
             pltpu.SemaphoreType.DMA((blk_devs, 2)),
             pltpu.SemaphoreType.DMA,
             pltpu.SemaphoreType.DMA((blk_devs,)),
-            pltpu.SemaphoreType.DMA,
+            pltpu.SemaphoreType.DMA((2,)),
             pltpu.SemaphoreType.DMA,
             pltpu.SemaphoreType.DMA,
             pltpu.SemaphoreType.DMA,
@@ -553,14 +655,14 @@
     return pl.pallas_call(
         product_kernel,
         out_shape=jax.ShapeDtypeStruct((FREQ_DEV, 2, count, width), jnp.float32),
-        in_specs=[pl.BlockSpec(memory_space=pltpu.VMEM)] * 3,
+        in_specs=[pl.BlockSpec(memory_space=pltpu.VMEM)] * 4,
         out_specs=pl.BlockSpec(memory_space=pl.ANY),
         scratch_shapes=[
-            pltpu.VMEM((FREQ_DEV, 2 * count, width), jnp.float32),
-            pltpu.SemaphoreType.DMA((FREQ_DEV, 2)),
+            pltpu.VMEM((FREQ_DEV, 2 * count, width // 2), jnp.float32),
+            pltpu.SemaphoreType.DMA((2, FREQ_DEV, 2)),
         ],
         compiler_params=pltpu.CompilerParams(vmem_limit_bytes=limit),
-    )(received, lefts, sorter)
+    )(early, received, lefts, sorter)
 
 
 def solution(mesh):

time: 21.6 us -> 21.5 us (level)
  the two profiles are of different devices: /device:TPU:5 before, /device:TPU:0 now
where the time goes in v5:
time: 21.5 us; the launch traced here: 21.2 us
  Pallas kernels  21.2 us (99%)
    pallas_call x1, Pallas kernels, per_device(): pl.pallas_call(functools.partial(send_kernel, freq_devs, blk_devs, col_st...  17.8 us
    pallas_call x1, Pallas kernels, per_device(): pl.pallas_call(product_kernel, out_shape=jax.ShapeDtypeStruct((FREQ_DEV,...  3.44 us

profile of v5, /device:TPU:0, one launch (start us, length us, event | category | flops | bytes accessed | tf_op | source)
XLA Modules:
  0.0 21.2 jit_solution(9401913837298717168)
XLA Ops:
  0.0 17.8 %shard_map.46 = (bf16[32,2,16,256]{3,2,1,0:T(8,128)(2,1)S(1)}, bf16[4,512,128]{2,1,0:T(8,128)(2,1)S(1)}, bf16[512,512]{1,0:T(8,128)(2,1)S(1)}, f32[4,512,512]{2,1,0:T(8,128)S(1)}) custom-call(s32[2]{0:T(128)} %band_hbm.1, f32[1,128]{1,0:T(1,128)} %bitcast.5, s32[1,256]{1,0:T(1,128)} %bitcast.4, bf16[32,128,1024]{2,1,0:T(8,128)(2,1)} %bitcast.3), custom_call_target="tpu_custom_call" | custom-call | tf_op jit(solution)/shard_map/pallas_call | solution.py:605
  17.8 3.4 %shard_map.47 = f32[4,2,256,1024]{3,2,1,0:T(8,128)} custom-call(f32[4,512,512]{2,1,0:T(8,128)S(1)} %get-tuple-element.9.early_ref, bf16[32,2,16,256]{3,2,1,0:T(8,128)(2,1)S(1)} %get-tuple-element.10.recv_ref, bf16[4,512,128]{2,1,0:T(8,128)(2,1)S(1)} %get-tuple-element.11.left_ref, bf16[512,512]{1,0:T(8,128)(2,1)S(1)} %get-tuple-element.12.sort_ref), custom_call_target="tpu_custom_call" | custom-call | tf_op jit(solution)/shard_map/pallas_call | solution.py:655

commit v6 on v5

--- a/solution.py
+++ b/solution.py
@@ -15,6 +15,7 @@
 VMEM_LARGE = 52 * 2**20
 GROUP = 32
 UNROLL = True
+EARLY = 2
 MESH = pl.DeviceIdType.MESH
 
 
@@ -138,7 +139,7 @@
 
     def send(step, part, some=None):
         first = 1 if step == blk_devs - 1 else 0
-        turn = me_f if first else me_f * jnp.minimum(blocks[step], 1)
+        turn = me_f if first else me_f * (blocks[step] // side)
 
         start, stop = some or (first, freq_devs)
 
@@ -328,14 +329,6 @@
 
     @pl.when(me_b < side)
     def _():
-        send(tail, 0)
-        send(2, 0)
-        send(1, 1)
-        send(2, 1)
-
-
-    @pl.when(me_b == side)
-    def _():
         send(2, 0, (0, 2))
         send(2, 1, (0, 2))
         send(2, 0, (2, freq_devs))
@@ -344,11 +337,20 @@
         send(1, 1)
 
 
+    @pl.when(me_b == side)
+    def _():
+        send(1, 1)
+        send(2, 0, (0, 2))
+        send(2, 1, (0, 2))
+        send(2, 0, (2, freq_devs))
+        send(2, 1, (2, freq_devs))
+        send(tail, 0)
+
+
     @pl.when(last)
     def _():
         send(tail, 0)
         send(1, 1)
-        send(2, 0)
 
     for step in range(3, tail):
         for part in range(2):
@@ -367,6 +369,7 @@
     def _():
         arrived(outgoing.at[0], send_sem.at[0])
         arrived(outgoing.at[1], send_sem.at[1])
+        send(2, 0)
         arrived(outgoing.at[2, :, 0], send_sem.at[2])
         send(2, 1)
 
@@ -384,10 +387,10 @@
     with jax.named_scope("first_part"):
         wait_part(0)
     with jax.named_scope("product"):
-        for i in range(FREQ_DEV):
+        for i in range(EARLY):
             rights = sorted_part(sort_ref, recv_ref, i, 0)
             for o in range(2):
-                product(left_ref, rights, i, o, early_ref)
+                product(left_ref, rights, i, o, early_ref.at[i])
     with jax.named_scope("send_wait"):
         arrived(near_in.at[pl.ds(0, freq_devs - 1)], near_send)
         arrived(plane_ref.at[pl.ds(0, blk_devs - 1)], plane_send)
@@ -430,7 +433,7 @@
     scale = 1.0 / math.sqrt(depth // 2)
     left = left_ref[i, pl.ds(o * count, count), :depth]
     for h, right in enumerate(rights):
-        out_ref[i, pl.ds(o * count, count), pl.ds(h * lanes, lanes)] = dot(left, right) * scale
+        out_ref[pl.ds(o * count, count), pl.ds(h * lanes, lanes)] = dot(left, right) * scale
 
 
 def fill_table(band_ref, fir_ref, table, freq_count):
@@ -557,29 +560,34 @@
 
 
 def product_kernel(early_ref, recv_ref, left_ref, sort_ref, out_ref, made, sems):
-    half = made.shape[2]
-    count = made.shape[1] // 2
+    half = made.shape[3]
+    count = made.shape[2] // 2
 
     def write(source, i, o, part):
         return pltpu.make_async_copy(
-            source.at[i, pl.ds(o * count, count)],
+            source.at[pl.ds(o * count, count)],
             out_ref.at[i, o, :, pl.ds(part * half, half)],
             sems.at[part, i, o],
         )
 
+    def source(i, part):
+        return early_ref.at[i] if part == 0 and i < EARLY else made.at[part, i]
+
+    for i in range(EARLY):
+        for o in range(2):
+            write(source(i, 0), i, o, 0).start()
     for i in range(FREQ_DEV):
-        for o in range(2):
-            write(early_ref, i, o, 0).start()
+        for part in range(2):
+            if part or i >= EARLY:
+                rights = sorted_part(sort_ref, recv_ref, i, part)
+                for o in range(2):
+                    product(left_ref, rights, i, o, made.at[part, i])
+                    write(made.at[part, i], i, o, part).start()
+
     for i in range(FREQ_DEV):
-        rights = sorted_part(sort_ref, recv_ref, i, 1)
-        for o in range(2):
-            product(left_ref, rights, i, o, made)
-            write(made, i, o, 1).start()
-
-    for part, source in enumerate((early_ref, made)):
-        for i in range(FREQ_DEV):
+        for part in range(2):
             for o in range(2):
-                write(source, i, o, part).wait()
+                write(source(i, part), i, o, part).wait()
 
 
 def per_device(traces, fir, targets, band):
@@ -608,7 +616,7 @@
             pltpu.VMEM((n, 2, ROWS, lanes), jnp.bfloat16),
             pltpu.VMEM((FREQ_DEV, 2 * count, wide), jnp.bfloat16),
             pltpu.VMEM((lines, GROUP * ROWS), jnp.bfloat16),
-            pltpu.VMEM((FREQ_DEV, 2 * count, width // 2), jnp.float32),
+            pltpu.VMEM((EARLY, 2 * count, width // 2), jnp.float32),
         ],
         in_specs=[pl.BlockSpec(memory_space=pl.ANY)] * 4,
         out_specs=[pl.BlockSpec(memory_space=pltpu.VMEM)] * 4,
@@ -658,7 +666,7 @@
         in_specs=[pl.BlockSpec(memory_space=pltpu.VMEM)] * 4,
         out_specs=pl.BlockSpec(memory_space=pl.ANY),
         scratch_shapes=[
-            pltpu.VMEM((FREQ_DEV, 2 * count, width // 2), jnp.float32),
+            pltpu.VMEM((2, FREQ_DEV, 2 * count, width // 2), jnp.float32),
             pltpu.SemaphoreType.DMA((2, FREQ_DEV, 2)),
         ],
         compiler_params=pltpu.CompilerParams(vmem_limit_bytes=limit),

time: 21.5 us -> 21.3 us (level)
  the two profiles are of different devices: /device:TPU:0 before, /device:TPU:9 now
where the time goes in v6:
time: 21.3 us; the launch traced here: 21.1 us
  Pallas kernels  21.1 us (99%)
    pallas_call x1, Pallas kernels, per_device(): pl.pallas_call(functools.partial(send_kernel, freq_devs, blk_devs, col_st...  17.7 us
    pallas_call x1, Pallas kernels, per_device(): pl.pallas_call(product_kernel, out_shape=jax.ShapeDtypeStruct((FREQ_DEV,...  3.44 us

profile of v6, /device:TPU:9, one launch (start us, length us, event | category | flops | bytes accessed | tf_op | source)
XLA Modules:
  0.0 21.1 jit_solution(6553919792002353352)
XLA Ops:
  0.0 17.7 %shard_map.46 = (bf16[32,2,16,256]{3,2,1,0:T(8,128)(2,1)S(1)}, bf16[4,512,128]{2,1,0:T(8,128)(2,1)S(1)}, bf16[512,512]{1,0:T(8,128)(2,1)S(1)}, f32[2,512,512]{2,1,0:T(8,128)S(1)}) custom-call(s32[2]{0:T(128)} %band_hbm.1, f32[1,128]{1,0:T(1,128)} %bitcast.5, s32[1,256]{1,0:T(1,128)} %bitcast.4, bf16[32,128,1024]{2,1,0:T(8,128)(2,1)} %bitcast.3), custom_call_target="tpu_custom_call" | custom-call | tf_op jit(solution)/shard_map/pallas_call | solution.py:613
  17.7 3.4 %shard_map.47 = f32[4,2,256,1024]{3,2,1,0:T(8,128)} custom-call(f32[2,512,512]{2,1,0:T(8,128)S(1)} %get-tuple-element.9.early_ref, bf16[32,2,16,256]{3,2,1,0:T(8,128)(2,1)S(1)} %get-tuple-element.10.recv_ref, bf16[4,512,128]{2,1,0:T(8,128)(2,1)S(1)} %get-tuple-element.11.left_ref, bf16[512,512]{1,0:T(8,128)(2,1)S(1)} %get-tuple-element.12.sort_ref), custom_call_target="tpu_custom_call" | custom-call | tf_op jit(solution)/shard_map/pallas_call | solution.py:663
